TPU v7x, 32 devices: a whole 2x2x4 slice. The times are simulated.
32 devices in a mesh: section: 2 (over core), dp: 4 (over z), tensor: 4 (over y, x).
Axes of the slice: x: 2, y: 2, z: 4, core: 2. Of those that a mesh axis runs over, the one named last changes fastest.
Arguments:
- inputs: bfloat16 [4, 2048, 768], P(None, 'dp'), may hold values from -6 to 6
- out_grad: bfloat16 [4, 2048, 768], P(None, 'dp'), may hold values from -6 to 6
- items: int32 [2, 4, 2048], P('section', None, 'dp'), may hold values from 0 to 5, never falling along the last dimension, each value on 1 to 1024 neighbouring positions
- send_order: int32 [2, 4, 4, 512], P('section', None, 'dp'), may hold values from 0 to 511, each once within a row
- recv_order: int32 [2, 4, 4, 512], P('section', None, 'dp'), may hold values from 0 to 511, each once within a row
- attn_weight: bfloat16 [2, 768, 3, 768], P('section', None, None, 'tensor'), may hold values from -0.21875 to 0.21875
- qv_bias: float32 [2, 2, 768], P('section', None, 'tensor'), may hold values from -3 to 3
- out_weight: bfloat16 [2, 768, 768], P('section', 'tensor'), may hold values from -0.625 to 0.625
- out_bias: float32 [2, 768], P('section'), may hold values from -3 to 3
- norm_first: float32 [2, 2, 768], P('section'), may hold values from 0.25 to 1.75
- up_weight: bfloat16 [2, 768, 3072], P('section', None, 'tensor'), may hold values from -0.21875 to 0.21875
- up_bias: float32 [2, 3072], P('section', 'tensor'), may hold values from -3 to 3
- down_weight: bfloat16 [2, 3072, 768], P('section', 'tensor'), may hold values from -0.109375 to 0.109375
- down_bias: float32 [2, 768], P('section'), may hold values from -3 to 3
- norm_second: float32 [2, 2, 768], P('section'), may hold values from 0.25 to 1.75
Outputs:
- activations: bfloat16 [2, 4, 2048, 768], P('section', None, 'dp')
- input_grads: float32 [2, 4, 2048, 768], P('section', None, 'dp')
- entropy_log: float32 [2, 4, 16, 12], P('section', None, 'dp', 'tensor')
- occupancy_log: float32 [2, 4, 16, 6], P('section', None, 'dp')
- attn_weight_grad: float32 [2, 768, 3, 768], P('section', 'dp', None, 'tensor')
- qv_bias_grad: float32 [2, 2, 768], P('section', None, 'tensor')
- out_weight_grad: float32 [2, 768, 768], P('section', 'tensor', 'dp')
- out_bias_grad: float32 [2, 768], P('section')
- norm_first_grad: float32 [2, 2, 768], P('section')
- up_weight_grad: float32 [2, 768, 3072], P('section', 'dp', 'tensor')
- up_bias_grad: float32 [2, 3072], P('section', 'tensor')
- down_weight_grad: float32 [2, 3072, 768], P('section', 'tensor', 'dp')
- down_bias_grad: float32 [2, 768], P('section')
- norm_second_grad: float32 [2, 2, 768], P('section')
Inputs may be any that keep to these rules, and one draw needn't show every extreme that they name: Each row of items[s, m] numbers the items of the cluster slots and never falls. `send_order`: each row holds every position of one device's 512 tokens once. `recv_order`: each row holds every received position of one device once.
All inputs are finite; a program needn't handle non-finite values.
Results may differ from a plain program's by a relative error of at most 0.034.
Values may be sent and summed in bfloat16 or wider, within the bound.
A program may use at most 256 MiB of HBM per device.

v0:
```python
import jax
import jax.numpy as jnp
from jax import lax
from jax.sharding import PartitionSpec as P

HEAD_DIM = 64
CLUSTER = 128
ITEMS = 6


EPSILON = 1e-06


def from_behind(block, axis, distance):
    devices = range(lax.axis_size(axis))
    route = [(i - distance, i) for i in devices if i - distance in devices]
    return lax.ppermute(block, axis, route)


def norm_rows(values, gain, shift):
    centre = jnp.mean(values, axis=-1, keepdims=True)
    spread = values - centre
    second = jnp.mean(spread * spread, axis=-1, keepdims=True)
    return spread * lax.rsqrt(second + EPSILON) * gain + shift


def inverse_of(order):
    count = order.shape[0]
    return jnp.zeros((count,), jnp.int32).at[order].set(jnp.arange(count, dtype=jnp.int32))


def masked_scores(queries, keys_all, labels, scale):
    scores = (
        jnp.einsum("cqhe,ckhe->chqk", queries, keys_all, preferred_element_type=jnp.float32) * scale
    )
    same_item = labels[:, None, :, None] == labels[:, None, None, :]
    masked = jnp.where(same_item, scores, -1e30)
    row_peak = jnp.max(masked, axis=-1, keepdims=True)
    shifted = jnp.exp(masked - row_peak)
    row_total = jnp.sum(shifted, axis=-1, keepdims=True)
    return (shifted / row_total, masked - row_peak, row_total, same_item)


def attend_forward(queries, keys_all, values, labels, scale):
    attn_prob, centred, row_total, same_item = masked_scores(queries, keys_all, labels, scale)
    inner = jnp.sum(jnp.where(same_item, attn_prob * centred, 0.0), axis=-1)
    entropy = jnp.mean(jnp.log(row_total[..., 0]) - inner, axis=-1)
    mixed_rows = jnp.einsum(
        "chqk,ckhe->cqhe",
        attn_prob.astype(jnp.bfloat16),
        values,
        preferred_element_type=jnp.float32,
    )
    return (mixed_rows.astype(jnp.bfloat16), entropy)


def attend_backward(queries, keys_all, values, grad_mixed, labels, scale):
    attn_prob = masked_scores(queries, keys_all, labels, scale)[0]
    grad_values = jnp.einsum(
        "chqk,cqhe->ckhe",
        attn_prob.astype(jnp.bfloat16),
        grad_mixed,
        preferred_element_type=jnp.float32,
    )
    grad_prob = jnp.einsum(
        "cqhe,ckhe->chqk", grad_mixed, values, preferred_element_type=jnp.float32
    )
    grad_score = attn_prob * (grad_prob - jnp.sum(attn_prob * grad_prob, axis=-1, keepdims=True))
    grad_low = grad_score.astype(jnp.bfloat16)
    grad_queries = (
        jnp.einsum("chqk,ckhe->cqhe", grad_low, keys_all, preferred_element_type=jnp.float32)
        * scale
    )
    grad_keys = (
        jnp.einsum("chqk,cqhe->ckhe", grad_low, queries, preferred_element_type=jnp.float32) * scale
    )
    return jnp.stack([grad_queries, grad_keys, grad_values], axis=2).astype(jnp.bfloat16)


def shards(
    inputs,
    out_grad,
    items,
    send_order,
    recv_order,
    attn_weight,
    qv_bias,
    out_weight,
    out_bias,
    norm_first,
    up_weight,
    up_bias,
    down_weight,
    down_bias,
    norm_second,
):
    micro_count = inputs.shape[0]
    row_count = inputs.shape[1]
    width = inputs.shape[2]
    heads_here = attn_weight.shape[3] // HEAD_DIM
    clusters_here = row_count // CLUSTER
    scale = HEAD_DIM ** (-0.5)
    is_first = lax.axis_index("section") == 0
    w_attn = attn_weight[0]
    w_out = out_weight[0]
    w_up = up_weight[0]
    w_down = down_weight[0]
    bias_three = jnp.stack([qv_bias[0, 0], jnp.zeros_like(qv_bias[0, 0]), qv_bias[0, 1]])
    b_out = out_bias[0]
    b_up = up_bias[0]
    b_down = down_bias[0]
    norm_one = norm_first[0]
    norm_two = norm_second[0]
    sends = send_order[0, :, 0]
    recvs = recv_order[0, :, 0]
    labels_all = items[0]
    kept_input, kept_proj, kept_cluster, kept_mixed = ([], [], [], [])
    kept_resid, kept_hidden, kept_upward, kept_active, kept_second = ([], [], [], [], [])
    results, entropies = ([], [])
    arrived = jnp.zeros((row_count, width), jnp.bfloat16)
    for tick in range(micro_count + 1):
        early = min(tick, micro_count - 1)
        late = max(tick - 1, 0)
        rows_in = jnp.where(is_first, inputs[early], arrived)
        send_idx = jnp.where(is_first, sends[early], sends[late])
        recv_idx = jnp.where(is_first, recvs[early], recvs[late])
        labels = jnp.where(is_first, labels_all[early], labels_all[late]).reshape(
            clusters_here, CLUSTER
        )
        recv_back = inverse_of(recv_idx)
        send_back = inverse_of(send_idx)
        projected = (
            jnp.einsum("td,dsf->tsf", rows_in, w_attn, preferred_element_type=jnp.float32)
            + bias_three
        )
        proj_low = projected.astype(jnp.bfloat16)
        outgoing = jnp.take(proj_low, send_idx, axis=0).reshape(row_count, 3, heads_here, HEAD_DIM)
        arrived_qkv = lax.all_to_all(outgoing, "dp", split_axis=0, concat_axis=0, tiled=True)
        count_heads = arrived_qkv.shape[2]
        forward_grouped = jnp.take(arrived_qkv, recv_idx, axis=0)
        forward_shaped = forward_grouped.reshape(clusters_here, CLUSTER, 3, count_heads, HEAD_DIM)
        mixed_rows, entropy = attend_forward(
            forward_shaped[:, :, 0], forward_shaped[:, :, 1], forward_shaped[:, :, 2], labels, scale
        )
        forward_home_rows = jnp.take(
            mixed_rows.reshape(row_count, count_heads, HEAD_DIM), recv_back, axis=0
        )
        forward_returned = lax.all_to_all(
            forward_home_rows, "dp", split_axis=0, concat_axis=0, tiled=True
        )
        restored = jnp.take(forward_returned, send_back, axis=0)
        restored, entropy, clustered = (
            restored,
            entropy,
            jnp.transpose(forward_grouped, (0, 2, 1, 3)),
        )
        mixed_tok = restored.reshape(row_count, heads_here * HEAD_DIM)
        attended = (
            lax.psum(jnp.dot(mixed_tok, w_out, preferred_element_type=jnp.float32), "tensor")
            + b_out
        )
        residual = rows_in.astype(jnp.float32) + attended
        hidden = norm_rows(residual, norm_one[0], norm_one[1])
        upward = (
            jnp.dot(hidden.astype(jnp.bfloat16), w_up, preferred_element_type=jnp.float32) + b_up
        )
        active = jax.nn.gelu(upward).astype(jnp.bfloat16)
        branch = (
            lax.psum(jnp.dot(active, w_down, preferred_element_type=jnp.float32), "tensor") + b_down
        )
        second = hidden + branch
        result = norm_rows(second, norm_two[0], norm_two[1]).astype(jnp.bfloat16)
        kept_input.append(rows_in)
        kept_proj.append(proj_low)
        kept_cluster.append(clustered)
        kept_mixed.append(mixed_tok)
        kept_resid.append(residual)
        kept_hidden.append(hidden)
        kept_upward.append(upward)
        kept_active.append(active)
        kept_second.append(second)
        results.append(result)
        entropies.append(entropy)
        if tick < micro_count:
            arrived = from_behind(result, "section", 1)
    grad_attn = jnp.zeros(w_attn.shape, jnp.float32)
    grad_qv = jnp.zeros((2, w_attn.shape[2]), jnp.float32)
    grad_out = jnp.zeros(w_out.shape, jnp.float32)
    grad_out_bias = jnp.zeros((width,), jnp.float32)
    grad_norm_one = jnp.zeros((2, width), jnp.float32)
    grad_up = jnp.zeros(w_up.shape, jnp.float32)
    grad_up_bias = jnp.zeros((w_up.shape[1],), jnp.float32)
    grad_down = jnp.zeros(w_down.shape, jnp.float32)
    grad_down_bias = jnp.zeros((width,), jnp.float32)
    grad_norm_two = jnp.zeros((2, width), jnp.float32)
    in_grads = []
    grad_arrived = jnp.zeros((row_count, width), jnp.bfloat16)
    for tick in range(micro_count + 1):
        before = max(tick - 1, 0)
        after = min(tick + 1, micro_count)
        micro_low = max(tick - 1, 0)
        micro_high = min(tick, micro_count - 1)

        def pick(stored):
            return jnp.where(is_first, stored[before], stored[after])

        live = jnp.where(
            is_first, 1.0 if tick >= 1 else 0.0, 1.0 if tick <= micro_count - 1 else 0.0
        )
        send_idx = jnp.where(is_first, sends[micro_low], sends[micro_high])
        recv_idx = jnp.where(is_first, recvs[micro_low], recvs[micro_high])
        labels = jnp.where(is_first, labels_all[micro_low], labels_all[micro_high]).reshape(
            clusters_here, CLUSTER
        )
        recv_back = inverse_of(recv_idx)
        send_back = inverse_of(send_idx)
        upstream = jnp.where(is_first, grad_arrived, out_grad[micro_high]).astype(jnp.float32)
        rows_in = pick(kept_input)
        mixed_tok = pick(kept_mixed)
        residual = pick(kept_resid)
        hidden = pick(kept_hidden)
        upward = pick(kept_upward)
        active = pick(kept_active)
        second = pick(kept_second)
        norm_pair = jax.vjp(norm_rows, second, norm_two[0], norm_two[1])
        grad_second, gain_two, shift_two = norm_pair[1](upstream)
        d_branch = grad_second.astype(jnp.bfloat16)
        grad_down_bias = grad_down_bias + live * jnp.sum(d_branch.astype(jnp.float32), axis=0)
        grad_down = grad_down + live * jnp.einsum(
            "tf,td->fd", active, d_branch, preferred_element_type=jnp.float32
        )
        grad_active = jnp.einsum("td,fd->tf", d_branch, w_down, preferred_element_type=jnp.float32)
        gelu_pair = jax.vjp(jax.nn.gelu, upward)
        d_up = gelu_pair[1](grad_active)[0].astype(jnp.bfloat16)
        grad_up_bias = grad_up_bias + live * jnp.sum(d_up.astype(jnp.float32), axis=0)
        grad_up = grad_up + live * jnp.einsum(
            "td,tf->df", hidden.astype(jnp.bfloat16), d_up, preferred_element_type=jnp.float32
        )
        from_units = jnp.einsum("tf,df->td", d_up, w_up, preferred_element_type=jnp.float32)
        d_hidden = grad_second + lax.psum(from_units.astype(jnp.bfloat16), "tensor").astype(
            jnp.float32
        )
        first_pair = jax.vjp(norm_rows, residual, norm_one[0], norm_one[1])
        d_resid, gain_one, shift_one = first_pair[1](d_hidden)
        d_att = d_resid.astype(jnp.bfloat16)
        grad_out_bias = grad_out_bias + live * jnp.sum(d_att.astype(jnp.float32), axis=0)
        grad_out = grad_out + live * jnp.einsum(
            "tf,td->fd", mixed_tok, d_att, preferred_element_type=jnp.float32
        )
        d_mixed = jnp.einsum("td,fd->tf", d_att, w_out, preferred_element_type=jnp.float32).astype(
            jnp.bfloat16
        )
        d_sent = jnp.take(d_mixed, send_idx, axis=0).reshape(row_count, 1, heads_here, HEAD_DIM)
        proj_sent = jnp.take(pick(kept_proj), send_idx, axis=0).reshape(
            row_count, 3, heads_here, HEAD_DIM
        )
        bundle = lax.all_to_all(
            jnp.concatenate([proj_sent, d_sent], axis=1),
            "dp",
            split_axis=0,
            concat_axis=0,
            tiled=True,
        )
        grouped = jnp.take(bundle, recv_idx, axis=0)
        qkv_grouped = grouped[:, :3]
        dout_grouped = grouped[:, 3]
        shaped = qkv_grouped.reshape(clusters_here, CLUSTER, 3, heads_here, HEAD_DIM)
        grad_cl = attend_backward(
            shaped[:, :, 0],
            shaped[:, :, 1],
            shaped[:, :, 2],
            dout_grouped.reshape(clusters_here, CLUSTER, heads_here, HEAD_DIM),
            labels,
            scale,
        )
        home_rows = jnp.take(grad_cl.reshape(row_count, 3, heads_here, HEAD_DIM), recv_back, axis=0)
        returned = lax.all_to_all(home_rows, "dp", split_axis=0, concat_axis=0, tiled=True)
        d_proj = jnp.take(returned, send_back, axis=0).reshape(row_count, 3, heads_here * HEAD_DIM)
        grad_attn = grad_attn + live * jnp.einsum(
            "td,tsf->dsf", rows_in, d_proj, preferred_element_type=jnp.float32
        )
        column_sums = jnp.sum(d_proj.astype(jnp.float32), axis=0)
        grad_qv = grad_qv + live * jnp.stack([column_sums[0], column_sums[2]])
        grad_norm_one = grad_norm_one + live * jnp.stack([gain_one, shift_one])
        grad_norm_two = grad_norm_two + live * jnp.stack([gain_two, shift_two])
        from_heads = jnp.einsum("tsf,dsf->td", d_proj, w_attn, preferred_element_type=jnp.float32)
        d_input = d_resid + lax.psum(from_heads.astype(jnp.bfloat16), "tensor").astype(jnp.float32)
        in_grads.append(d_input)
        if tick < micro_count:
            grad_arrived = from_behind(d_input.astype(jnp.bfloat16), "section", -1)
    matrices = (
        lax.psum_scatter(
            grad_attn.astype(jnp.bfloat16), "dp", scatter_dimension=0, tiled=True
        ).astype(jnp.float32),
        lax.psum_scatter(
            grad_out.astype(jnp.bfloat16), "dp", scatter_dimension=1, tiled=True
        ).astype(jnp.float32),
        lax.psum_scatter(
            grad_up.astype(jnp.bfloat16), "dp", scatter_dimension=0, tiled=True
        ).astype(jnp.float32),
        lax.psum_scatter(
            grad_down.astype(jnp.bfloat16), "dp", scatter_dimension=1, tiled=True
        ).astype(jnp.float32),
    )
    smalls = lax.psum(
        (grad_qv, grad_out_bias, grad_norm_one, grad_up_bias, grad_down_bias, grad_norm_two), "dp"
    )
    activations = jnp.where(is_first, jnp.stack(results[:micro_count]), jnp.stack(results[1:]))
    input_grads = jnp.where(is_first, jnp.stack(in_grads[1:]), jnp.stack(in_grads[:micro_count]))
    entropy_log = jnp.where(is_first, jnp.stack(entropies[:micro_count]), jnp.stack(entropies[1:]))
    item_numbers = jnp.arange(ITEMS, dtype=jnp.int32)
    labels_grid = labels_all.reshape(micro_count, clusters_here, CLUSTER)
    occupancy_log = jnp.sum((labels_grid[..., None] == item_numbers).astype(jnp.float32), axis=2)
    return (
        activations[None],
        input_grads[None],
        entropy_log[None],
        occupancy_log[None],
        matrices[0][None],
        smalls[0][None],
        matrices[1][None],
        smalls[1][None],
        smalls[2][None],
        matrices[2][None],
        smalls[3][None],
        matrices[3][None],
        smalls[4][None],
        smalls[5][None],
    )


def solution(mesh):
    return jax.shard_map(
        shards,
        mesh=mesh,
        in_specs=(
            P(None, "dp", None),
            P(None, "dp", None),
            P("section", None, "dp"),
            P("section", None, "dp", None),
            P("section", None, "dp", None),
            P("section", None, None, "tensor"),
            P("section", None, "tensor"),
            P("section", "tensor", None),
            P("section", None),
            P("section", None, None),
            P("section", None, "tensor"),
            P("section", "tensor"),
            P("section", "tensor", None),
            P("section", None),
            P("section", None, None),
        ),
        out_specs=(
            P("section", None, "dp", None),
            P("section", None, "dp", None),
            P("section", None, "dp", "tensor"),
            P("section", None, "dp", None),
            P("section", "dp", None, "tensor"),
            P("section", None, "tensor"),
            P("section", "tensor", "dp"),
            P("section", None),
            P("section", None, None),
            P("section", "dp", "tensor"),
            P("section", "tensor"),
            P("section", "tensor", "dp"),
            P("section", None),
            P("section", None, None),
        ),
        check_vma=False,
    )
```

profile of v0, /device:TPU:0, one launch (start us, length us, event | category | flops | bytes accessed | tf_op | source)
XLA Modules:
  0.0 2487.7 jit_solution(16322492185689362144)
XLA Ops:
  78.4 59.5 %all-reduce.22.cloned.1.call-done = f32[512,768]{1,0:T(8,128)} async-done(((f32[512,768]{1,0:T(8,128)}), f32[512,768]{1,0:T(8,128)}) %all-reduce.22.cloned.1.call-update) | async-done | bytes 1572880 | tf_op jit(solution)/shard_map/psum | solution.py:159
  146.8 60.3 %all-reduce.24.cloned.1.call-done = f32[512,768]{1,0:T(8,128)} async-done(((f32[512,768]{1,0:T(8,128)}), f32[512,768]{1,0:T(8,128)}) %all-reduce.24.cloned.1.call-update) | async-done | bytes 1572880 | tf_op jit(solution)/shard_map/psum | solution.py:169
  249.2 13.0 all-to-all-done.2
  315.9 58.4 %all-reduce.26.cloned.1.call-done = f32[512,768]{1,0:T(8,128)} async-done(((f32[512,768]{1,0:T(8,128)}), f32[512,768]{1,0:T(8,128)}) %all-reduce.26.cloned.1.call-update) | async-done | bytes 1572880 | tf_op jit(solution)/shard_map/psum | solution.py:159
  388.0 61.1 %all-reduce.28.cloned.1.call-done = f32[512,768]{1,0:T(8,128)} async-done(((f32[512,768]{1,0:T(8,128)}), f32[512,768]{1,0:T(8,128)}) %all-reduce.28.cloned.1.call-update) | async-done | bytes 1572880 | tf_op jit(solution)/shard_map/psum | solution.py:169
  501.4 13.0 all-to-all-done.4
  577.4 49.0 %all-reduce.30.cloned.1.call-done = f32[512,768]{1,0:T(8,128)} async-done(((f32[512,768]{1,0:T(8,128)}), f32[512,768]{1,0:T(8,128)}) %all-reduce.30.cloned.1.call-update) | async-done | bytes 1572880 | tf_op jit(solution)/shard_map/psum | solution.py:159
  657.4 21.0 all-reduce.42.cloned.1.call-done
  681.9 60.5 %all-reduce.32.cloned.1.call-done = f32[512,768]{1,0:T(8,128)} async-done(((f32[512,768]{1,0:T(8,128)}), f32[512,768]{1,0:T(8,128)}) %all-reduce.32.cloned.1.call-update) | async-done | bytes 1572880 | tf_op jit(solution)/shard_map/psum | solution.py:169
  779.8 10.0 all-to-all-done.10
  858.5 13.8 all-to-all-done.11
  897.3 41.6 %all-reduce.44.cloned.1.call-done = bf16[512,768]{1,0:T(8,128)(2,1)} async-done(((bf16[512,768]{1,0:T(8,128)(2,1)}), bf16[512,768]{1,0:T(8,128)(2,1)}) %all-reduce.44.cloned.1.call-update) | async-done | bytes 786448 | tf_op jit(solution)/shard_map/psum | solution.py:287
  1071.7 45.9 %all-reduce.34.cloned.1.call-done = f32[512,768]{1,0:T(8,128)} async-done(((f32[512,768]{1,0:T(8,128)}), f32[512,768]{1,0:T(8,128)}) %all-reduce.34.cloned.1.call-update) | async-done | bytes 1572880 | tf_op jit(solution)/shard_map/psum | solution.py:159
  1156.9 12.6 all-reduce.46.cloned.1.call-done
  1173.1 60.5 %all-reduce.36.cloned.1.call-done = f32[512,768]{1,0:T(8,128)} async-done(((f32[512,768]{1,0:T(8,128)}), f32[512,768]{1,0:T(8,128)}) %all-reduce.36.cloned.1.call-update) | async-done | bytes 1572880 | tf_op jit(solution)/shard_map/psum | solution.py:169
  1264.1 16.9 all-to-all-done.12
  1350.2 12.9 all-to-all-done.13
  1385.4 44.7 %all-reduce.48.cloned.1.call-done = bf16[512,768]{1,0:T(8,128)(2,1)} async-done(((bf16[512,768]{1,0:T(8,128)(2,1)}), bf16[512,768]{1,0:T(8,128)(2,1)}) %all-reduce.48.cloned.1.call-update) | async-done | bytes 786448 | tf_op jit(solution)/shard_map/psum | solution.py:287
  1487.7 11.3 all-to-all-done.8
  1553.7 39.0 %all-reduce.38.cloned.1.call-done = f32[512,768]{1,0:T(8,128)} async-done(((f32[512,768]{1,0:T(8,128)}), f32[512,768]{1,0:T(8,128)}) %all-reduce.38.cloned.1.call-update) | async-done | bytes 1572880 | tf_op jit(solution)/shard_map/psum | solution.py:159
  1621.6 23.1 all-reduce.50.cloned.1.call-done
  1648.3 60.3 %all-reduce.40.cloned.1.call-done = f32[512,768]{1,0:T(8,128)} async-done(((f32[512,768]{1,0:T(8,128)}), f32[512,768]{1,0:T(8,128)}) %all-reduce.40.cloned.1.call-update) | async-done | bytes 1572880 | tf_op jit(solution)/shard_map/psum | solution.py:169
  1745.0 11.5 all-to-all-done.14
  1872.5 36.5 %all-reduce.52.cloned.1.call-done = bf16[512,768]{1,0:T(8,128)(2,1)} async-done(((bf16[512,768]{1,0:T(8,128)(2,1)}), bf16[512,768]{1,0:T(8,128)(2,1)}) %all-reduce.52.cloned.1.call-update) | async-done | bytes 786448 | tf_op jit(solution)/shard_map/psum | solution.py:287
  1936.0 39.4 %all-reduce.54.cloned.1.call-done = bf16[512,768]{1,0:T(8,128)(2,1)} async-done(((bf16[512,768]{1,0:T(8,128)(2,1)}), bf16[512,768]{1,0:T(8,128)(2,1)}) %all-reduce.54.cloned.1.call-update) | async-done | bytes 786448 | tf_op jit(solution)/shard_map/psum | solution.py:240
  2133.0 45.5 %all-reduce.56.cloned.1.call-done = bf16[512,768]{1,0:T(8,128)(2,1)} async-done(((bf16[512,768]{1,0:T(8,128)(2,1)}), bf16[512,768]{1,0:T(8,128)(2,1)}) %all-reduce.56.cloned.1.call-update) | async-done | bytes 786448 | tf_op jit(solution)/shard_map/psum | solution.py:287
  2204.8 42.7 %all-reduce.58.cloned.1.call-done = bf16[512,768]{1,0:T(8,128)(2,1)} async-done(((bf16[512,768]{1,0:T(8,128)(2,1)}), bf16[512,768]{1,0:T(8,128)(2,1)}) %all-reduce.58.cloned.1.call-update) | async-done | bytes 786448 | tf_op jit(solution)/shard_map/psum | solution.py:240
  2307.3 14.4 all-to-all-done.18
  2368.0 12.2 all-to-all-done.19
  2415.5 17.5 all-reduce
  2433.1 14.2 all-reduce.60.cloned.1.call-done
  2455.3 23.4 reduce-scatter.9.cloned.1.call-done
  (1602 shorter events, 1422.5 us)
Async XLA Ops:
  23.1 22.2 all-to-all-start
  64.7 73.2 %all-reduce.22.cloned.1.call-start = ((), (), s32[]{:S(2)}) async-start(), calls=%async_computation.24 | async-start | bytes 3145728 | tf_op jit(solution)/shard_map/psum | solution.py:159
  78.1 129.0 %all-reduce.24.cloned.1.call-start = ((), (), s32[]{:S(2)}) async-start(), calls=%async_computation.25 | async-start | bytes 3145728 | tf_op jit(solution)/shard_map/psum | solution.py:169
  297.3 77.1 %all-reduce.26.cloned.1.call-start = ((), (), s32[]{:S(2)}) async-start(), calls=%async_computation.26 | async-start | bytes 3145728 | tf_op jit(solution)/shard_map/psum | solution.py:159
  315.5 133.5 %all-reduce.28.cloned.1.call-start = ((), (), s32[]{:S(2)}) async-start(), calls=%async_computation.27 | async-start | bytes 3145728 | tf_op jit(solution)/shard_map/psum | solution.py:169
  549.3 77.1 %all-reduce.30.cloned.1.call-start = ((), (), s32[]{:S(2)}) async-start(), calls=%async_computation.28 | async-start | bytes 3145728 | tf_op jit(solution)/shard_map/psum | solution.py:159
  567.6 110.8 %all-reduce.42.cloned.1.call-start = ((), (), s32[]{:S(2)}) async-start(), calls=%async_computation.34 | async-start | bytes 1572864 | tf_op jit(solution)/shard_map/psum | solution.py:240
  576.9 165.5 %all-reduce.32.cloned.1.call-start = ((), (), s32[]{:S(2)}) async-start(), calls=%async_computation.29 | async-start | bytes 3145728 | tf_op jit(solution)/shard_map/psum | solution.py:169
  764.8 25.0 %all-to-all-start.10 = ((bf16[4,2,49152]{2,1,0:T(2,128)(2,1)}), bf16[4,2,49152]{2,1,0:T(2,128)(2,1)}, u32[]{:S(2)}, u32[]{:S(2)}) async-start(bf16[4,2,49152]{2,1,0:T(2,128)(2,1)} %reshape.2502), calls=%async_computation.10 | async-start | bytes 1572864 | tf_op jit(solution)/shard_map/all_to_all | solution.py:257
  856.8 82.2 %all-reduce.44.cloned.1.call-start = ((), (), s32[]{:S(2)}) async-start(), calls=%async_computation.35 | async-start | bytes 1572864 | tf_op jit(solution)/shard_map/psum | solution.py:287
  1040.5 77.1 %all-reduce.34.cloned.1.call-start = ((), (), s32[]{:S(2)}) async-start(), calls=%async_computation.30 | async-start | bytes 3145728 | tf_op jit(solution)/shard_map/psum | solution.py:159
  1058.8 110.8 %all-reduce.46.cloned.1.call-start = ((), (), s32[]{:S(2)}) async-start(), calls=%async_computation.36 | async-start | bytes 1572864 | tf_op jit(solution)/shard_map/psum | solution.py:240
  1071.7 161.9 %all-reduce.36.cloned.1.call-start = ((), (), s32[]{:S(2)}) async-start(), calls=%async_computation.31 | async-start | bytes 3145728 | tf_op jit(solution)/shard_map/psum | solution.py:169
  1256.5 24.5 all-to-all-start.12
  1347.7 82.4 %all-reduce.48.cloned.1.call-start = ((), (), s32[]{:S(2)}) async-start(), calls=%async_computation.37 | async-start | bytes 1572864 | tf_op jit(solution)/shard_map/psum | solution.py:287
  1477.3 21.7 all-to-all-start.8
  1520.3 72.4 %all-reduce.38.cloned.1.call-start = ((), (), s32[]{:S(2)}) async-start(), calls=%async_computation.32 | async-start | bytes 3145728 | tf_op jit(solution)/shard_map/psum | solution.py:159
  1533.7 111.0 %all-reduce.50.cloned.1.call-start = ((), (), s32[]{:S(2)}) async-start(), calls=%async_computation.38 | async-start | bytes 1572864 | tf_op jit(solution)/shard_map/psum | solution.py:240
  1553.7 154.9 %all-reduce.40.cloned.1.call-start = ((), (), s32[]{:S(2)}) async-start(), calls=%async_computation.33 | async-start | bytes 3145728 | tf_op jit(solution)/shard_map/psum | solution.py:169
  1731.7 24.8 all-to-all-start.14
  1826.8 82.2 %all-reduce.52.cloned.1.call-start = ((), (), s32[]{:S(2)}) async-start(), calls=%async_computation.39 | async-start | bytes 1572864 | tf_op jit(solution)/shard_map/psum | solution.py:287
  1862.0 113.4 %all-reduce.54.cloned.1.call-start = ((), (), s32[]{:S(2)}) async-start(), calls=%async_computation.40 | async-start | bytes 1572864 | tf_op jit(solution)/shard_map/psum | solution.py:240
  2000.4 25.1 %all-to-all-start.16 = ((bf16[4,2,49152]{2,1,0:T(2,128)(2,1)}), bf16[4,2,49152]{2,1,0:T(2,128)(2,1)}, u32[]{:S(2)}, u32[]{:S(2)}) async-start(bf16[4,2,49152]{2,1,0:T(2,128)(2,1)} %reshape.2514), calls=%async_computation.16 | async-start | bytes 1572864 | tf_op jit(solution)/shard_map/all_to_all | solution.py:257
  2096.0 82.5 %all-reduce.56.cloned.1.call-start = ((), (), s32[]{:S(2)}) async-start(), calls=%async_computation.41 | async-start | bytes 1572864 | tf_op jit(solution)/shard_map/psum | solution.py:287
  2131.2 116.3 %all-reduce.58.cloned.1.call-start = ((), (), s32[]{:S(2)}) async-start(), calls=%async_computation.42 | async-start | bytes 1572864 | tf_op jit(solution)/shard_map/psum | solution.py:240
  2197.8 202.5 %reduce-scatter.13.cloned.1.call-start = ((), (), s32[]{:S(2)}) async-start(), calls=%async_computation.46 | async-start | bytes 491520
  2255.7 152.3 %reduce-scatter.15.cloned.1.call-start = ((), (), s32[]{:S(2)}) async-start(), calls=%async_computation.47 | async-start | bytes 1474560
  2286.7 35.1 %all-to-all-start.18 = ((bf16[4,2,49152]{2,1,0:T(2,128)(2,1)}), bf16[4,2,49152]{2,1,0:T(2,128)(2,1)S(1)}, u32[]{:S(2)}, u32[]{:S(2)}) async-start(bf16[4,2,49152]{2,1,0:T(2,128)(2,1)} %reshape.2518), calls=%async_computation.18 | async-start | bytes 1572864 | tf_op jit(solution)/shard_map/all_to_all | solution.py:257
  2291.3 120.8 %reduce-scatter.11.cloned.1.call-start = ((), (), s32[]{:S(2)}) async-start(), calls=%async_computation.45 | async-start | bytes 1474560 | tf_op jit(solution)/shard_map/reduce_scatter | solution.py:298
  2359.7 20.5 all-to-all-start.19
  2364.1 83.2 %all-reduce.60.cloned.1.call-start = ((), (), s32[]{:S(2)}) async-start(), calls=%async_computation.43 | async-start | bytes 1572864 | tf_op jit(solution)/shard_map/psum | solution.py:287
  2399.4 79.4 %reduce-scatter.9.cloned.1.call-start = ((), (), s32[]{:S(2)}) async-start(), calls=%async_computation.44 | async-start | bytes 1474560 | tf_op jit(solution)/shard_map/reduce_scatter | solution.py:292
  (406 other events, 3763.3 us)
Sparse Core Ops, SparseCore 0:
  78.2 59.6 all-reduce.21
  146.2 60.8 all-reduce.23
  315.6 58.6 all-reduce.25
  388.1 60.8 all-reduce.27
  567.7 58.6 all-reduce.29
  629.6 48.7 all-reduce.41
  681.5 60.8 all-reduce.31
  892.1 46.8 all-reduce.43
  1058.9 58.6 all-reduce.33
  1120.8 48.7 all-reduce.45
  1172.6 60.8 all-reduce.35
  1383.2 46.8 all-reduce.47
  1533.8 58.8 all-reduce.37
  1596.0 48.7 all-reduce.49
  1647.7 60.8 all-reduce.39
  1862.1 46.8 all-reduce.51
  1926.7 48.7 all-reduce.53
  2131.3 47.1 all-reduce.55
  2197.9 49.5 all-reduce.57
  2255.8 20.5 reduce-scatter.12
  2278.7 36.6 reduce-scatter.14
  2317.7 31.4 reduce-scatter.10
  2399.5 47.7 all-reduce.59
  2449.5 29.1 reduce-scatter.8
where the time goes:
time: 2500 us; the launch traced here: 2490 us
  waiting for transfers between devices  1100 us (44%)
  local copies, waits for them, and re-layouts  666 us (27%)
  other arithmetic  374 us (15%)
  matrix products  201 us (8%)
  starting transfers between devices  107 us (4%)
    psum x5, waiting for transfers between devices, shards(): lax.psum(jnp.dot(active, w_down, preferred_element_type=jnp.float32), 'te...  303 us
    psum x5, waiting for transfers between devices, shards(): lax.psum(jnp.dot(mixed_tok, w_out, preferred_element_type=jnp.float32), '...  252 us
    unnamed x848, local copies, waits for them, and re-layouts  214 us
    psum x5, waiting for transfers between devices, shards(): lax.psum(from_heads.astype(jnp.bfloat16), 'tensor').astype(jnp.float32)  182 us
    psum x5, waiting for transfers between devices, shards(): lax.psum(from_units.astype(jnp.bfloat16), 'tensor').astype(jnp.float32)  139 us
    all_to_all x5, waiting for transfers between devices, shards(): lax.all_to_all(jnp.concatenate([proj_sent, d_sent], axis=1), 'dp', split_...  61.2 us
    all_to_all x5, waiting for transfers between devices, shards(): lax.all_to_all(outgoing, 'dp', split_axis=0, concat_axis=0, tiled=True)  54 us
  transfers between devices with their start and end apart: 52, of which 45 were waited for; matrix products, arithmetic and copies ran while one was open for 17% of the time, Pallas kernels for 0%

commit v1 on v0

v1 whole, which is shorter than its diff:
```python
import functools

import jax
import jax.numpy as jnp
from jax import lax
from jax.experimental import pallas as pl
from jax.experimental.pallas import tpu as pltpu
from jax.sharding import PartitionSpec as P

HEAD_DIM = 64
CLUSTER = 128
ITEMS = 6
EPSILON = 1e-06
MESH = pl.DeviceIdType.MESH
VMEM_LIMIT = 60 * 1024 * 1024
bf16 = jnp.bfloat16
f32 = jnp.float32


def nn(a, b):
    return lax.dot_general(a, b, (((1,), (0,)), ((), ())), preferred_element_type=f32)


def nt(a, b):
    return lax.dot_general(a, b, (((1,), (1,)), ((), ())), preferred_element_type=f32)


def tn(a, b):
    return lax.dot_general(a, b, (((0,), (0,)), ((), ())), preferred_element_type=f32)


def loop(count, body):
    def step(index, carry):
        body(index)
        return carry

    lax.fori_loop(0, count, step, 0)


def rows_at(index, size):
    return pl.ds(pl.multiple_of(index * size, size), size)


class Place:
    def __init__(self, n_z, n_t, rows):
        self.n_z, self.n_t, self.rows = n_z, n_t, rows
        self.z, self.t = lax.axis_index("dp"), lax.axis_index("tensor")
        self.piece = rows // n_z
        self.own = rows // n_t
        self.chunk = max(self.piece, 128)
        self.chunks = rows // self.chunk
        self.per_chunk = self.chunk // self.piece

    def greet(self):
        barrier = pltpu.get_barrier_semaphore()

        def greet_z(k):
            peer = lax.rem(self.z + 1 + k, self.n_z)
            pl.semaphore_signal(barrier, inc=1, device_id={"dp": peer}, device_id_type=MESH)

        def greet_t(k):
            peer = lax.rem(self.t + 1 + k, self.n_t)
            pl.semaphore_signal(barrier, inc=1, device_id={"tensor": peer}, device_id_type=MESH)

        loop(self.n_z - 1, greet_z)
        loop(self.n_t - 1, greet_t)
        pl.semaphore_wait(barrier, self.n_z + self.n_t - 2)

    def own_rows(self):
        return rows_at(self.t, self.own)

    def z_copy(self, m, k, src, dst, sems):
        peer = lax.rem(self.z + k, self.n_z)
        return pltpu.make_async_remote_copy(
            src_ref=src.at[m, rows_at(peer, self.piece)],
            dst_ref=dst.at[m, rows_at(self.z, self.piece)],
            send_sem=sems[0].at[m, k - 1],
            recv_sem=sems[1].at[m, k - 1],
            device_id={"dp": peer},
            device_id_type=MESH,
        )

    def z_chunk(self, kk):
        return lax.rem(self.z // self.per_chunk + 1 + kk, self.chunks)

    def z_send_chunk(self, m, cc, src, dst, sems):
        def one(j):
            peer = cc * self.per_chunk + j
            k = lax.rem(peer - self.z + self.n_z, self.n_z)

            @pl.when(k > 0)
            def _():
                self.z_copy(m, k, src, dst, sems).start()

        loop(self.per_chunk, one)

    def z_keep_own(self, m, src, dst):
        mine = rows_at(self.z, self.piece)
        dst[m, mine] = src[m, mine]

    def z_wait(self, m, src, dst, sems):
        loop(self.n_z - 1, lambda k: self.z_copy(m, k + 1, src, dst, sems).wait())

    def sum_copy(self, m, k, src, dst, sems):
        peer = lax.rem(self.t + k, self.n_t)
        return pltpu.make_async_remote_copy(
            src_ref=src.at[m, k - 1],
            dst_ref=dst.at[m, k - 1],
            send_sem=sems[0].at[m, k - 1],
            recv_sem=sems[1].at[m, k - 1],
            device_id={"tensor": peer},
            device_id_type=MESH,
        )

    def sum_put(self, m, k, part, src, dst, sems, mine):
        @pl.when(k > 0)
        def _():
            src[m, k - 1] = part.astype(bf16)
            self.sum_copy(m, k, src, dst, sems).start()

        @pl.when(k == 0)
        def _():
            mine[m] = part

    def sum_take(self, m, src, dst, sems, mine):
        total = mine[m]
        for k in range(1, self.n_t):
            self.sum_copy(m, k, src, dst, sems).wait()
        for k in range(1, self.n_t):
            total = total + dst[m, k - 1].astype(f32)
        return total

    def gather_copy(self, m, k, buf, sems):
        peer = lax.rem(self.t + k, self.n_t)
        return pltpu.make_async_remote_copy(
            src_ref=buf.at[m, self.own_rows()],
            dst_ref=buf.at[m, self.own_rows()],
            send_sem=sems[0].at[m, k - 1],
            recv_sem=sems[1].at[m, k - 1],
            device_id={"tensor": peer},
            device_id_type=MESH,
        )

    def gather_start(self, m, buf, sems):
        loop(self.n_t - 1, lambda k: self.gather_copy(m, k + 1, buf, sems).start())

    def gather_wait_from(self, m, k, buf, sems):
        @pl.when(k > 0)
        def _():
            self.gather_copy(m, self.n_t - k, buf, sems).wait_recv()

    def gather_wait_sent(self, m, buf, sems):
        loop(self.n_t - 1, lambda k: self.gather_copy(m, k + 1, buf, sems).wait_send())

    def gather_wait(self, m, buf, sems):
        loop(self.n_t - 1, lambda k: self.gather_copy(m, k + 1, buf, sems).wait())


def pick_rows(column, count):
    return (lax.broadcasted_iota(jnp.int32, (column.shape[0], count), 1) == column).astype(bf16)


def place_rows(row, first, count):
    numbers = lax.broadcasted_iota(jnp.int32, (count, row.shape[1]), 0) + first
    return (numbers == row).astype(bf16)


def by_head(block, heads):
    lane = lax.broadcasted_iota(jnp.int32, block.shape, 1) // HEAD_DIM
    return jnp.concatenate([jnp.where(lane == h, block, jnp.zeros_like(block)) for h in range(heads)])


def fold_heads(stacked, heads):
    count = stacked.shape[0] // heads
    lane = lax.broadcasted_iota(jnp.int32, (count, stacked.shape[1]), 1) // HEAD_DIM
    total = jnp.where(lane == 0, stacked[:count], 0.0)
    for h in range(1, heads):
        total = jnp.where(lane == h, stacked[h * count : (h + 1) * count], total)
    return total


def softmax_parts(scores, same):
    masked = jnp.where(same, scores, -1e30)
    centred = masked - jnp.max(masked, axis=-1, keepdims=True)
    grown = jnp.exp(centred)
    total = jnp.sum(grown, axis=-1, keepdims=True)
    return grown / total, centred, total


def normalise(values):
    centre = jnp.mean(values, axis=-1, keepdims=True)
    spread = values - centre
    second = jnp.mean(spread * spread, axis=-1, keepdims=True)
    inverse = lax.rsqrt(second + EPSILON)
    return spread * inverse, inverse


def norm_backward(grad, normed, inverse, gain):
    scaled = grad * gain
    first = jnp.mean(scaled, axis=-1, keepdims=True)
    second = jnp.mean(scaled * normed, axis=-1, keepdims=True)
    return inverse * (scaled - first - normed * second)


def forward_kernel(
    n_z, n_t, heads,
    x, send_col, send_row, recv_col, recv_row, label_col, label_row,
    wa, ba, wo, bo, norm1, wu, bu, wd, bd, norm2,
    xp, grouped, ms, n1, inv1, hfull, act, gprime, n2, inv2, ent, x_next,
    zsend, zrecv, mixc, msend, rs1_src, rs1_dst, mine1, hid, rs2_src, rs2_dst, mine2, out_sent,
    q_s, q_r, m_s, m_r, r1_s, r1_r, g1_s, g1_r, r2_s, r2_r, g2_s, g2_r,
):
    rows = x.shape[1]
    at = Place(n_z, n_t, rows)
    width = heads * HEAD_DIM
    scale = HEAD_DIM**-0.5
    q_sems, m_sems, r1_sems, g1_sems, r2_sems, g2_sems = (
        (q_s, q_r), (m_s, m_r), (r1_s, r1_r), (g1_s, g1_r), (r2_s, r2_r), (g2_s, g2_r),
    )
    at.greet()

    def project(m):
        def chunk(kk):
            cc = at.z_chunk(kk)
            here = rows_at(cc, at.chunk)
            moved = nn(pick_rows(send_col[m, here], rows), x[m]).astype(bf16)
            xp[m, here] = moved
            zsend[m, here] = (nn(moved, wa[...]) + ba[...]).astype(bf16)
            at.z_send_chunk(m, cc, zsend, zrecv, q_sems)

        loop(at.chunks, chunk)
        at.z_keep_own(m, zsend, zrecv)

    def attend(m):
        at.z_wait(m, zsend, zrecv, q_sems)
        ent[m] = jnp.zeros(ent.shape[1:], f32)

        def cluster(c):
            here = rows_at(c, CLUSTER)
            block = nn(pick_rows(recv_col[m, here], rows), zrecv[m]).astype(bf16)
            grouped[m, here] = block
            queries, keys, values = (block[:, i * width : (i + 1) * width] for i in range(3))
            scores = nt(queries, by_head(keys, heads)) * scale
            same = label_col[m, here] == label_row[m, :, here]
            probs = []
            lane = lax.broadcasted_iota(jnp.int32, (1, 128), 1)
            log_row = jnp.zeros((1, 128), f32)
            for h in range(heads):
                prob, centred, total = softmax_parts(
                    scores[:, h * CLUSTER : (h + 1) * CLUSTER], same
                )
                inner = jnp.sum(jnp.where(same, prob * centred, 0.0), axis=-1, keepdims=True)
                entropy = jnp.mean(jnp.log(total) - inner, axis=0, keepdims=True)
                log_row = jnp.where(lane == h, entropy, log_row)
                probs.append(prob.astype(bf16))
            ent[m, pl.ds(c, 1)] = log_row
            mixed = nn(jnp.concatenate(probs, axis=1), by_head(values, heads))
            mixc[m, here] = mixed.astype(bf16)

        loop(rows // CLUSTER, cluster)

        def home(kk):
            cc = at.z_chunk(kk)
            here = rows_at(cc, at.chunk)
            one_hot = place_rows(recv_row[m], cc * at.chunk, at.chunk)
            msend[m, here] = nn(one_hot, mixc[m]).astype(bf16)
            at.z_send_chunk(m, cc, msend, ms, m_sems)

        loop(at.chunks, home)
        at.z_keep_own(m, msend, ms)

    def out_project(m):
        at.z_wait(m, msend, ms, m_sems)

        def part(kk):
            k = lax.rem(kk + 1, n_t)
            here = rows_at(lax.rem(at.t + k, n_t), at.own)
            at.sum_put(m, k, nn(ms[m, here], wo[...]), rs1_src, rs1_dst, r1_sems, mine1)

        loop(n_t, part)

    def first_norm(m):
        total = at.sum_take(m, rs1_src, rs1_dst, r1_sems, mine1) + bo[...]
        here = at.own_rows()
        normed, inverse = normalise(xp[m, here].astype(f32) + total)
        hidden = normed * norm1[0:1] + norm1[1:2]
        n1[m] = normed
        inv1[m] = jnp.broadcast_to(inverse, inv1.shape[1:])
        hid[m] = hidden
        hfull[m, here] = hidden.astype(bf16)
        at.gather_start(m, hfull, g1_sems)

    def feed(m):
        def part(k):
            at.gather_wait_from(m, k, hfull, g1_sems)
            here = rows_at(lax.rem(at.t + k, n_t), at.own)
            up = nn(hfull[m, here], wu[...]) + bu[...]
            square = up * up
            tanh = jnp.tanh(0.7978845608028654 * up * (1.0 + 0.044715 * square))
            half = 0.5 * (1.0 + tanh)
            slope = 0.7978845608028654 * (1.0 + 3 * 0.044715 * square)
            gprime[m, here] = (half + 0.5 * up * (1.0 - tanh * tanh) * slope).astype(bf16)
            active = (up * half).astype(bf16)
            act[m, here] = active
            at.sum_put(m, k, nn(active, wd[...]), rs2_src, rs2_dst, r2_sems, mine2)

        loop(n_t, part)

    def second_norm(m):
        total = at.sum_take(m, rs2_src, rs2_dst, r2_sems, mine2) + bd[...]
        here = at.own_rows()
        normed, inverse = normalise(hid[m] + total)
        n2[m] = normed
        inv2[m] = jnp.broadcast_to(inverse, inv2.shape[1:])
        out_sent[m, here] = (normed * norm2[0:1] + norm2[1:2]).astype(bf16)
        at.gather_start(m, out_sent, g2_sems)

    def back_to_tokens(m):
        at.gather_wait(m, out_sent, g2_sems)

        def chunk(cc):
            one_hot = place_rows(send_row[m], cc * 128, 128)
            x_next[m, rows_at(cc, 128)] = nn(one_hot, out_sent[m]).astype(bf16)

        loop(rows // 128, chunk)
        at.gather_wait_sent(m, hfull, g1_sems)

    project(0)
    project(1)
    attend(0)
    out_project(0)
    attend(1)
    first_norm(0)
    feed(0)
    out_project(1)
    second_norm(0)
    first_norm(1)
    feed(1)
    back_to_tokens(0)
    second_norm(1)
    back_to_tokens(1)


def backward_kernel(
    n_z, n_t, heads,
    grad, send_col, send_row, recv_col, recv_row, label_col, label_row,
    wa, wo, norm1, wu, wd, norm2,
    xp, grouped, ms, n1, inv1, hfull, act, gprime, n2, inv2,
    grad_next, g_attn, g_up, g_down, g_out, g_vec,
    db, dup, dsec, rs1_src, rs1_dst, mine1, dres, da, dmsend, dmrecv, dgc, dqsend, dproj,
    rs2_src, rs2_dst, mine2, din,
    a1_s, a1_r, r1_s, r1_r, a2_s, a2_r, m_s, m_r, q_s, q_r, r2_s, r2_r, a3_s, a3_r,
):
    rows = grad.shape[1]
    at = Place(n_z, n_t, rows)
    width = heads * HEAD_DIM
    scale = HEAD_DIM**-0.5
    a1_sems, r1_sems, a2_sems, m_sems, q_sems, r2_sems, a3_sems = (
        (a1_s, a1_r), (r1_s, r1_r), (a2_s, a2_r), (m_s, m_r), (q_s, q_r), (r2_s, r2_r), (a3_s, a3_r),
    )
    at.greet()
    g_vec[...] = jnp.zeros(g_vec.shape, f32)

    def add_vec(index, value):
        g_vec[index : index + 1, : value.shape[1]] += value

    def column_sum(value):
        return jnp.sum(value.astype(f32), axis=0, keepdims=True)

    def add_to(ref, m, value):
        if m == 0:
            ref[...] = value
        else:
            ref[...] += value

    def second_norm(m):
        here = at.own_rows()
        up = nn(pick_rows(send_col[m, here], rows), grad[m])
        normed = n2[m]
        down = norm_backward(up, normed, inv2[m][:, :1], norm2[0:1])
        dsec[m] = down
        low = down.astype(bf16)
        db[m, here] = low
        at.gather_start(m, db, a1_sems)
        add_vec(0, column_sum(up * normed))
        add_vec(1, column_sum(up))
        add_vec(2, column_sum(low))

    def feed(m):
        def part(k):
            at.gather_wait_from(m, k, db, a1_sems)
            here = rows_at(lax.rem(at.t + k, n_t), at.own)
            low = (nt(db[m, here], wd[...]) * gprime[m, here].astype(f32)).astype(bf16)
            dup[m, here] = low
            at.sum_put(m, k, nt(low, wu[...]), rs1_src, rs1_dst, r1_sems, mine1)

        loop(n_t, part)

    def feed_weights(m):
        add_to(g_down, m, tn(db[m], act[m]))
        add_to(g_up, m, tn(hfull[m], dup[m]))
        add_vec(6, column_sum(dup[m]))

    def first_norm(m):
        total = at.sum_take(m, rs1_src, rs1_dst, r1_sems, mine1)
        here = at.own_rows()
        up = dsec[m] + total
        normed = n1[m]
        down = norm_backward(up, normed, inv1[m][:, :1], norm1[0:1])
        dres[m] = down
        low = down.astype(bf16)
        da[m, here] = low
        at.gather_start(m, da, a2_sems)
        add_vec(3, column_sum(up * normed))
        add_vec(4, column_sum(up))
        add_vec(5, column_sum(low))

    def out_back(m):
        at.gather_wait(m, da, a2_sems)

        def chunk(kk):
            cc = at.z_chunk(kk)
            here = rows_at(cc, at.chunk)
            dmsend[m, here] = nt(da[m, here], wo[...]).astype(bf16)
            at.z_send_chunk(m, cc, dmsend, dmrecv, m_sems)

        loop(at.chunks, chunk)
        at.z_keep_own(m, dmsend, dmrecv)

    def out_weights(m):
        add_to(g_out, m, tn(da[m], ms[m]))

    def attend(m):
        at.z_wait(m, dmsend, dmrecv, m_sems)

        def cluster(c):
            here = rows_at(c, CLUSTER)
            dmix = nn(pick_rows(recv_col[m, here], rows), dmrecv[m]).astype(bf16)
            block = grouped[m, here]
            queries, keys, values = (block[:, i * width : (i + 1) * width] for i in range(3))
            keys_by_head = by_head(keys, heads)
            scores = nt(queries, keys_by_head) * scale
            same = label_col[m, here] == label_row[m, :, here]
            dprob = nt(dmix, by_head(values, heads))
            probs, dscores = [], []
            for h in range(heads):
                cut = slice(h * CLUSTER, (h + 1) * CLUSTER)
                prob = softmax_parts(scores[:, cut], same)[0]
                outer = prob * dprob[:, cut]
                dscore = outer - prob * jnp.sum(outer, axis=-1, keepdims=True)
                probs.append(prob.astype(bf16))
                dscores.append(dscore.astype(bf16))
            prob_all = jnp.concatenate(probs, axis=1)
            dscore_all = jnp.concatenate(dscores, axis=1)
            dgc[m, here, 0:width] = (nn(dscore_all, keys_by_head) * scale).astype(bf16)
            dkeys = fold_heads(tn(dscore_all, queries), heads)
            dgc[m, here, width : 2 * width] = (dkeys * scale).astype(bf16)
            dgc[m, here, 2 * width : 3 * width] = fold_heads(tn(prob_all, dmix), heads).astype(bf16)

        loop(rows // CLUSTER, cluster)

        def home(kk):
            cc = at.z_chunk(kk)
            here = rows_at(cc, at.chunk)
            one_hot = place_rows(recv_row[m], cc * at.chunk, at.chunk)
            dqsend[m, here] = nn(one_hot, dgc[m]).astype(bf16)
            at.z_send_chunk(m, cc, dqsend, dproj, q_sems)

        loop(at.chunks, home)
        at.z_keep_own(m, dqsend, dproj)

    def in_project(m):
        at.z_wait(m, dqsend, dproj, q_sems)

        def part(kk):
            k = lax.rem(kk + 1, n_t)
            here = rows_at(lax.rem(at.t + k, n_t), at.own)
            at.sum_put(m, k, nt(dproj[m, here], wa[...]), rs2_src, rs2_dst, r2_sems, mine2)

        loop(n_t, part)

    def in_weights(m):
        add_to(g_attn, m, tn(xp[m], dproj[m]))
        add_vec(7, column_sum(dproj[m]))

    def layer_input(m):
        total = at.sum_take(m, rs2_src, rs2_dst, r2_sems, mine2)
        here = at.own_rows()
        din[m, here] = (dres[m] + total).astype(bf16)
        at.gather_start(m, din, a3_sems)

    def back_to_tokens(m):
        at.gather_wait(m, din, a3_sems)

        def chunk(cc):
            one_hot = place_rows(send_row[m], cc * 128, 128)
            grad_next[m, rows_at(cc, 128)] = nn(one_hot, din[m]).astype(bf16)

        loop(rows // 128, chunk)
        at.gather_wait_sent(m, db, a1_sems)

    second_norm(0)
    second_norm(1)
    feed(0)
    feed(1)
    first_norm(0)
    feed_weights(0)
    out_back(0)
    first_norm(1)
    feed_weights(1)
    attend(0)
    out_weights(0)
    out_back(1)
    in_project(0)
    attend(1)
    in_weights(0)
    layer_input(0)
    out_weights(1)
    in_project(1)
    back_to_tokens(0)
    in_weights(1)
    layer_input(1)
    back_to_tokens(1)


def dma_pair(count):
    return [pltpu.SemaphoreType.DMA((2, count)), pltpu.SemaphoreType.DMA((2, count))]


def call(kernel, outs, scratch, args, name, collective_id):
    vmem = pl.BlockSpec(memory_space=pltpu.VMEM)
    return pl.pallas_call(
        kernel,
        out_shape=[jax.ShapeDtypeStruct(shape, dtype) for shape, dtype in outs],
        in_specs=[vmem] * len(args),
        out_specs=[vmem] * len(outs),
        scratch_shapes=scratch,
        compiler_params=pltpu.CompilerParams(
            collective_id=collective_id, has_side_effects=True, vmem_limit_bytes=VMEM_LIMIT
        ),
        name=name,
    )(*args)


def shards(
    inputs, out_grad, items, send_order, recv_order,
    attn_weight, qv_bias, out_weight, out_bias, norm_first,
    up_weight, up_bias, down_weight, down_bias, norm_second,
):
    micros, rows, width = inputs.shape
    n_z, n_t, n_s = lax.axis_size("dp"), lax.axis_size("tensor"), lax.axis_size("section")
    cols = attn_weight.shape[3]
    heads = cols // HEAD_DIM
    hidden = up_weight.shape[2]
    half = micros // n_s
    clusters = rows // CLUSTER
    own = rows // n_t
    core = lax.axis_index("section")
    z, t = lax.axis_index("dp"), lax.axis_index("tensor")

    def both(value):
        return lax.all_gather(value[0], "section")

    def mine(value, axis):
        return lax.dynamic_slice_in_dim(value, core * half, half, axis)

    wa = both(attn_weight).reshape(2, width, 3 * cols)
    wo, wu, wd = both(out_weight), both(up_weight), both(down_weight)
    small = jnp.concatenate(
        [
            qv_bias[0].reshape(-1), out_bias[0], norm_first[0].reshape(-1), up_bias[0],
            down_bias[0], norm_second[0].reshape(-1),
        ]
    )
    smalls = lax.all_gather(small, "section")
    index = jnp.stack([items[0], send_order[0, :, 0], recv_order[0, :, 0]])
    index = mine(lax.all_gather(index, "section"), 2)

    def vectors(layer):
        row = smalls[layer]
        cuts = [2 * cols, width, 2 * width, hidden, width, 2 * width]
        parts, start = [], 0
        for cut in cuts:
            parts.append(row[start : start + cut])
            start += cut
        ba = jnp.concatenate([parts[0][:cols], jnp.zeros((cols,), f32), parts[0][cols:]])
        return (
            ba[None], parts[1][None], parts[2].reshape(2, width), parts[3][None], parts[4][None],
            parts[5].reshape(2, width),
        )

    def orders(layer):
        out = []
        for value in (index[layer, 1], index[layer, 2], index[layer, 0]):
            out += [value[:, :, None], value[:, None, :]]
        return out

    def forward(layer, x):
        ba, bo, norm1, bu, bd, norm2 = vectors(layer)
        pair = (half, rows)
        outs = [
            ((*pair, width), bf16), ((*pair, 3 * cols), bf16), ((*pair, cols), bf16),
            ((half, own, width), f32), ((half, own, 128), f32), ((*pair, width), bf16),
            ((*pair, hidden), bf16), ((*pair, hidden), bf16),
            ((half, own, width), f32), ((half, own, 128), f32),
            ((half, max(8, clusters), 128), f32), ((*pair, width), bf16),
        ]
        sums = (half, n_t - 1, own, width)
        scratch = [
            pltpu.VMEM((*pair, 3 * cols), bf16), pltpu.VMEM((*pair, 3 * cols), bf16),
            pltpu.VMEM((*pair, cols), bf16), pltpu.VMEM((*pair, cols), bf16),
            pltpu.VMEM(sums, bf16), pltpu.VMEM(sums, bf16), pltpu.VMEM((half, own, width), f32),
            pltpu.VMEM((half, own, width), f32),
            pltpu.VMEM(sums, bf16), pltpu.VMEM(sums, bf16), pltpu.VMEM((half, own, width), f32),
            pltpu.VMEM((*pair, width), bf16),
            *dma_pair(n_z - 1), *dma_pair(n_z - 1),
            *dma_pair(n_t - 1), *dma_pair(n_t - 1), *dma_pair(n_t - 1), *dma_pair(n_t - 1),
        ]
        args = [
            x, *orders(layer), wa[layer], ba, wo[layer], bo, norm1, wu[layer], bu, wd[layer], bd,
            norm2,
        ]
        kernel = functools.partial(forward_kernel, n_z, n_t, heads)
        return call(kernel, outs, scratch, args, "layer_forward", 0)

    def backward(layer, grad, kept):
        _, _, norm1, _, _, norm2 = vectors(layer)
        pair = (half, rows)
        outs = [
            ((*pair, width), bf16), ((width, 3 * cols), f32), ((width, hidden), f32),
            ((width, hidden), f32), ((width, cols), f32), ((8, max(width, hidden, 3 * cols)), f32),
        ]
        sums = (half, n_t - 1, own, width)
        scratch = [
            pltpu.VMEM((*pair, width), bf16), pltpu.VMEM((*pair, hidden), bf16),
            pltpu.VMEM((half, own, width), f32),
            pltpu.VMEM(sums, bf16), pltpu.VMEM(sums, bf16), pltpu.VMEM((half, own, width), f32),
            pltpu.VMEM((half, own, width), f32), pltpu.VMEM((*pair, width), bf16),
            pltpu.VMEM((*pair, cols), bf16), pltpu.VMEM((*pair, cols), bf16),
            pltpu.VMEM((*pair, 3 * cols), bf16), pltpu.VMEM((*pair, 3 * cols), bf16),
            pltpu.VMEM((*pair, 3 * cols), bf16),
            pltpu.VMEM(sums, bf16), pltpu.VMEM(sums, bf16), pltpu.VMEM((half, own, width), f32),
            pltpu.VMEM((*pair, width), bf16),
            *dma_pair(n_t - 1), *dma_pair(n_t - 1), *dma_pair(n_t - 1),
            *dma_pair(n_z - 1), *dma_pair(n_z - 1), *dma_pair(n_t - 1), *dma_pair(n_t - 1),
        ]
        args = [
            grad, *orders(layer), wa[layer], wo[layer], norm1, wu[layer], wd[layer], norm2, *kept,
        ]
        kernel = functools.partial(backward_kernel, n_z, n_t, heads)
        return call(kernel, outs, scratch, args, "layer_backward", 1)

    *kept0, ent0, x1 = forward(0, mine(inputs, 0))
    *kept1, ent1, x2 = forward(1, x1)
    grad1, *sums1 = backward(1, mine(out_grad, 0), kept1)
    grad0, *sums0 = backward(0, grad1, kept0)

    swap = [(0, 1), (1, 0)]

    def to_owner(first, second):
        kept = jnp.where(core == 0, first, second)
        came = lax.ppermute(jnp.where(core == 0, second, first), "section", swap)
        return jnp.where(
            core == 0, jnp.concatenate([kept, came]), jnp.concatenate([came, kept])
        )

    activations = to_owner(x1, x2)
    input_grads = to_owner(grad0, grad1).astype(f32)

    def reduced(first, second):
        both_layers = jnp.stack([first, second]).astype(bf16)
        both_layers = both_layers.reshape(n_s * n_z, first.shape[0] // n_z, first.shape[1])
        return lax.psum_scatter(
            both_layers, ("section", "dp"), scatter_dimension=0, tiled=False
        ).astype(f32)

    attn_grad = reduced(sums0[0], sums1[0]).reshape(-1, 3, cols)
    up_grad = reduced(sums0[1], sums1[1])
    down_grad = reduced(sums0[2], sums1[2]).T
    out_grad_w = reduced(sums0[3], sums1[3]).T

    vec = jnp.stack([sums0[4], sums1[4]])
    by_rows = vec[:, :6, :width].reshape(n_s, -1)
    by_cols = jnp.concatenate([vec[:, 6, :hidden], vec[:, 7, : 3 * cols]], axis=1)
    spot = (jnp.arange(n_t) == t).astype(f32)
    by_cols = (spot[None, :, None] * by_cols[:, None, :]).reshape(n_s, -1)
    entropy = jnp.stack([ent0, ent1])[:, :, :clusters, :heads]
    spot_core = (jnp.arange(n_s) == core).astype(f32)
    spot_z = (jnp.arange(n_z) == z).astype(f32)
    entropy = (
        entropy[:, None, :, None, :, None, :]
        * spot_core[None, :, None, None, None, None, None]
        * spot_z[None, None, None, :, None, None, None]
        * spot[None, None, None, None, None, :, None]
    ).reshape(n_s, -1)
    sizes = [by_rows.shape[1], by_cols.shape[1], entropy.shape[1]]
    totals = lax.psum(
        jnp.concatenate([by_rows, by_cols, entropy], axis=1), ("section", "dp", "tensor")
    )
    totals = lax.dynamic_slice_in_dim(totals, core, 1, 0)[0]
    rows_part = totals[: sizes[0]].reshape(6, width)
    cols_part = totals[sizes[0] : sizes[0] + sizes[1]].reshape(n_t, -1)
    cols_part = lax.dynamic_slice_in_dim(cols_part, t, 1, 0)[0]
    entropy = totals[sizes[0] + sizes[1] :].reshape(micros, n_z, clusters, n_t, heads)
    entropy = lax.dynamic_slice_in_dim(entropy, z, 1, 1)[:, 0]
    entropy = lax.dynamic_slice_in_dim(entropy, t, 1, 2)[:, :, 0]
    qkv_sums = cols_part[hidden:].reshape(3, cols)

    item_numbers = jnp.arange(ITEMS, dtype=jnp.int32)
    grid = items[0].reshape(micros, clusters, CLUSTER)
    occupancy = jnp.sum((grid[..., None] == item_numbers).astype(f32), axis=2)
    results = (
        activations, input_grads, entropy, occupancy, attn_grad,
        jnp.stack([qkv_sums[0], qkv_sums[2]]), out_grad_w, rows_part[5], rows_part[3:5], up_grad,
        cols_part[:hidden], down_grad, rows_part[2], rows_part[0:2],
    )
    return tuple(value[None] for value in results)


def solution(mesh):
    return jax.shard_map(
        shards,
        mesh=mesh,
        in_specs=(
            P(None, "dp", None),
            P(None, "dp", None),
            P("section", None, "dp"),
            P("section", None, "dp", None),
            P("section", None, "dp", None),
            P("section", None, None, "tensor"),
            P("section", None, "tensor"),
            P("section", "tensor", None),
            P("section", None),
            P("section", None, None),
            P("section", None, "tensor"),
            P("section", "tensor"),
            P("section", "tensor", None),
            P("section", None),
            P("section", None, None),
        ),
        out_specs=(
            P("section", None, "dp", None),
            P("section", None, "dp", None),
            P("section", None, "dp", "tensor"),
            P("section", None, "dp", None),
            P("section", "dp", None, "tensor"),
            P("section", None, "tensor"),
            P("section", "tensor", "dp"),
            P("section", None),
            P("section", None, None),
            P("section", "dp", "tensor"),
            P("section", "tensor"),
            P("section", "tensor", "dp"),
            P("section", None),
            P("section", None, None),
        ),
        check_vma=False,
    )
```

time: 2500 us -> 874 us (0.35)
  waiting for transfers between devices: 1100 us -> 298 us
  local copies, waits for them, and re-layouts: 666 us -> 47.4 us
  Pallas kernels: 0 us -> 475 us
  other arithmetic: 374 us -> 28.5 us
  matrix products: 201 us -> 0 us
  starting transfers between devices: 107 us -> 1 us
    psum x20 -> x1, waiting for transfers between devices: 876 us -> 101 us  [shards(): lax.psum(jnp.concatenate([by_rows, by_cols, entropy], axis=1), ('section'...]
    pallas_call x0 -> x4, Pallas kernels: none -> 475 us  [call(): pl.pallas_call(kernel, out_shape=[jax.ShapeDtypeStruct(shape, dtype) for...]
    unnamed x848 -> x74, local copies, waits for them, and re-layouts: 214 us -> 10 us
    all_to_all x20 -> x0, waiting for transfers between devices: 197 us -> none  [the longest x5 61.2 us: shards(): lax.all_to_all(jnp.concatenate([proj_sent, d_sent], axis=1), 'dp', split_...]
    dot_general x85 -> x0, matrix products: 181 us -> none  [the longest x5 25.4 us: shards(): jnp.einsum('td,tf->df', hidden.astype(jnp.bfloat16), d_up, preferred_elem...]
    gather x45 -> x0, local copies, waits for them, and re-layouts: 173 us -> none  [the longest x5 25.2 us: shards(): jnp.take(returned, send_back, axis=0)]
    reduce_scatter x2 -> x4, waiting for transfers between devices: 23.4 us -> 185 us  [reduced(): lax.psum_scatter(both_layers, ('section', 'dp'), scatter_dimension=0, til...]
    reduce_sum x83 -> x1, other arithmetic: 161 us -> 0.1 us  [shards(): occupancy = jnp.sum((grid[..., None] == item_numbers).astype(f32), axis=2)]
  transfers between devices with their start and end apart: 52 -> 10, of which waited for: 45 -> 6; matrix products, arithmetic and copies ran while one was open for 17% -> 7% of each run, Pallas kernels for 0% -> 0%
where the time goes in v1:
time: 874 us; the launch traced here: 871 us
  Pallas kernels  475 us (54%)
  waiting for transfers between devices  298 us (34%)
  local copies, waits for them, and re-layouts  47.4 us (5%)
  other arithmetic  28.5 us (3%)
  between operations  14.9 us (2%)
    pallas_call x4, Pallas kernels, call(): pl.pallas_call(kernel, out_shape=[jax.ShapeDtypeStruct(shape, dtype) for...  475 us
    reduce_scatter x4, waiting for transfers between devices, reduced(): lax.psum_scatter(both_layers, ('section', 'dp'), scatter_dimension=0, til...  185 us
    psum x1, waiting for transfers between devices, shards(): lax.psum(jnp.concatenate([by_rows, by_cols, entropy], axis=1), ('section'...  101 us
  transfers between devices with their start and end apart: 10, of which 6 were waited for; matrix products, arithmetic and copies ran while one was open for 7% of the time, Pallas kernels for 0%

profile of v1, /device:TPU:0, one launch (start us, length us, event | category | flops | bytes accessed | tf_op | source)
XLA Modules:
  0.0 871.0 jit_solution(4991380118645371783)
XLA Ops:
  9.6 1.9 all-gather
  15.0 2.0 all-gather.2
  24.5 2.4 all_gather.29
  26.9 3.3 constant_dynamic-slice_fusion.7
  31.7 1.8 fusion.6
  36.4 3.3 slice_bitcast_fusion
  39.7 10.2 %all-gather.9.cloned.1.call-done = bf16[2,768,768]{2,1,0:T(8,128)(2,1)} async-done(((bf16[1,768,768]{2,1,0:T(8,128)(2,1)}), bf16[2,768,768]{2,1,0:T(8,128)(2,1)}) %all-gather.9.cloned.1.call-update) | async-done | bytes 2359312 | tf_op jit(solution)/shard_map/all_gather | solution.py:562
  49.9 3.2 slice_bitcast_fusion.1
  53.1 126.4 %layer_forward.2 = (bf16[2,512,768]{2,1,0:T(8,128)(2,1)}, bf16[2,512,576]{2,1,0:T(8,128)(2,1)}, bf16[2,512,192]{2,1,0:T(8,128)(2,1)}, f32[2,128,768]{2,1,0:T(8,1...) custom-call(bf16[2,512,768]{2,1,0:T(8,128)(2,1)} %get-tuple-element., ...), custom_call_target="tpu_custom_call" | custom-call | tf_op jit(solution)/shard_map/layer_forward/pallas_call | solution.py:532
  179.5 120.9 %layer_forward.3 = (bf16[2,512,768]{2,1,0:T(8,128)(2,1)}, bf16[2,512,576]{2,1,0:T(8,128)(2,1)}, bf16[2,512,192]{2,1,0:T(8,128)(2,1)}, f32[2,128,768]{2,1,0:T(8,1...) custom-call(bf16[2,512,768]{2,1,0:T(8,128)(2,1)} %get-tuple-element., ...), custom_call_target="tpu_custom_call" | custom-call | tf_op jit(solution)/shard_map/layer_forward/pallas_call | solution.py:532
  300.4 116.9 %layer_backward.2 = (bf16[2,512,768]{2,1,0:T(8,128)(2,1)}, f32[768,576]{1,0:T(8,128)}, f32[768,768]{1,0:T(8,128)}, f32[768,768]{1,0:T(8,128)}, f32[768,192]{1,0:T(8,128)}, /*index=5*/f32[8,768]{1,0:T(8,128)}) custom-call(bf16[2,512,768]{2,1,0:T(8,128)(2,1)} %get-tuple-element.181.grad, s32[2,512,1]{2,1,0:T(8,128)} %copy.95.send_col, s32[2,1,512]{2,1,0:T(1,128)} %bitcast.144, ...), custom_call_target="tpu_custom_call" | custom-call | tf_op jit(solution)/shard_map/layer_backward/pallas_call | solution.py:532
  417.3 110.8 %layer_backward.3 = (bf16[2,512,768]{2,1,0:T(8,128)(2,1)}, f32[768,576]{1,0:T(8,128)}, f32[768,768]{1,0:T(8,128)}, f32[768,768]{1,0:T(8,128)}, f32[768,192]{1,0:T(8,128)}, /*index=5*/f32[8,768]{1,0:T(8,128)}) custom-call(bf16[2,512,768]{2,1,0:T(8,128)(2,1)} %get-tuple-element.62.grad, s32[2,512,1]{2,1,0:T(8,128)} %copy.91.send_col, s32[2,1,512]{2,1,0:T(1,128)} %bitcast.135, ...), custom_call_target="tpu_custom_call" | custom-call | tf_op jit(solution)/shard_map/layer_backward/pallas_call | solution.py:532
  534.9 1.8 convert_bitcast_fusion.5
  537.2 2.5 copy.109
  539.8 1.6 copy-done.5
  541.5 1.6 copy-done.3
  543.2 1.6 pad_maximum_fusion.1
  544.9 1.6 copy-done.4
  546.6 1.6 copy-done.2
  548.3 1.6 pad_maximum_fusion
  551.3 2.9 select_bitcast_fusion
  556.9 100.7 %all-reduce.2.cloned.1.call-done = f32[2,10752]{1,0:T(2,128)} async-done(((f32[2,10752]{1,0:T(2,128)}), f32[2,10752]{1,0:T(2,128)}) %all-reduce.2.cloned.1.call-update) | async-done | bytes 86032 | tf_op jit(solution)/shard_map/psum | solution.py:697
  664.3 31.3 %reduce-scatter.7.cloned.1.call-done = bf16[1,192,192]{1,2,0:T(8,128)(2,1)} async-done(((bf16[8,192,192]{1,2,0:T(8,128)(2,1)}), bf16[1,192,192]{1,2,0:T(8,128)(2,1)}) %reduce-scatter.7.cloned.1.call-update) | async-done | bytes 73744 | tf_op jit(solution)/shard_map/reduce_scatter | solution.py:673
  695.6 1.6 convert_bitcast_fusion.9
  697.2 4.4 fusion
  701.5 3.4 maximum_select_fusion
  705.0 46.0 %reduce-scatter.5.cloned.1.call-done = bf16[1,192,576]{1,2,0:T(8,128)(2,1)} async-done(((bf16[8,192,576]{1,2,0:T(8,128)(2,1)}), bf16[1,192,576]{1,2,0:T(8,128)(2,1)}) %reduce-scatter.5.cloned.1.call-update) | async-done | bytes 221200 | tf_op jit(solution)/shard_map/reduce_scatter | solution.py:673
  750.9 1.9 copy.111
  752.9 53.7 %reduce-scatter.11.cloned.1.call-done = bf16[1,192,768]{2,1,0:T(8,128)(2,1)} async-done(((bf16[8,192,768]{2,1,0:T(8,128)(2,1)}), bf16[1,192,768]{2,1,0:T(8,128)(2,1)}) %reduce-scatter.11.cloned.1.call-update) | async-done | bytes 294928 | tf_op jit(solution)/shard_map/reduce_scatter | solution.py:673
  806.5 1.8 convert_bitcast_fusion.6
  808.4 53.8 %reduce-scatter.9.cloned.1.call-done = bf16[1,192,768]{2,1,0:T(8,128)(2,1)} async-done(((bf16[8,192,768]{2,1,0:T(8,128)(2,1)}), bf16[1,192,768]{2,1,0:T(8,128)(2,1)}) %reduce-scatter.9.cloned.1.call-update) | async-done | bytes 294928 | tf_op jit(solution)/shard_map/reduce_scatter | solution.py:673
  862.1 1.8 convert_element_type.94
  (168 shorter events, 35.8 us)
Async XLA Ops:
  7.2 2.4 copy-start.21
  7.2 2.4 copy-start.20
  7.2 2.4 copy-start.17
  7.2 4.4 copy-start.27
  7.2 4.4 copy-start.22
  7.2 4.4 copy-start.24
  7.2 4.5 copy-start.25
  7.3 4.5 copy-start.26
  7.3 24.5 %all-gather.7.cloned.1.call-start = ((), (), s32[]{:S(2)}) async-start(), calls=%async_computation.4 | async-start | bytes 2654208 | tf_op jit(solution)/shard_map/all_gather | solution.py:562
  8.0 28.4 %all-gather.11.cloned.1.call-start = ((), (), s32[]{:S(2)}) async-start(), calls=%async_computation.6 | async-start | bytes 3538944 | tf_op jit(solution)/shard_map/all_gather | solution.py:562
  8.7 6.2 copy-start.23
  8.8 41.1 %all-gather.9.cloned.1.call-start = ((), (), s32[]{:S(2)}) async-start(), calls=%async_computation.5 | async-start | bytes 3538944 | tf_op jit(solution)/shard_map/all_gather | solution.py:562
  9.5 648.1 %all-reduce.2.cloned.1.call-start = ((), (), s32[]{:S(2)}) async-start(), calls=%async_computation.7 | async-start | bytes 172032 | tf_op jit(solution)/shard_map/psum | solution.py:697
  11.9 10.3 %copy-start.11 = (s32[1,1,2,512]{3,0,2,1:T(1,128)}, s32[1,1,2,512]{3,0,2,1:T(1,128)S(1)}, u32[]{:S(2)}) copy-start(s32[1,1,2,512]{3,0,2,1:T(1,128)S(1)} %copy.147) | copy-start | bytes 12292
  12.9 11.3 %copy-start.12 = (s32[1,1,2,512]{3,0,2,1:T(1,128)}, s32[1,1,2,512]{3,0,2,1:T(1,128)S(1)}, u32[]{:S(2)}) copy-start(s32[1,1,2,512]{3,0,2,1:T(1,128)S(1)} %copy.146) | copy-start | bytes 12292
  13.9 13.0 %copy-start.13 = (s32[1,1,2,512]{3,0,2,1:T(1,128)}, s32[1,1,2,512]{3,0,2,1:T(1,128)S(1)}, u32[]{:S(2)}) copy-start(s32[1,1,2,512]{3,0,2,1:T(1,128)S(1)} %copy.145) | copy-start | bytes 12292
  15.0 11.9 %copy-start.9 = (bf16[4,512,768]{2,1,0:T(8,128)(2,1)S(1)}, bf16[4,512,768]{2,1,0:T(8,128)(2,1)}, u32[]{:S(2)}) copy-start(bf16[4,512,768]{2,1,0:T(8,128)(2,1)} %param.16) | copy-start | bytes 9437188
  19.0 11.2 %copy-start.14 = (s32[1,1,2,512]{3,0,2,1:T(1,128)}, s32[1,1,2,512]{3,0,2,1:T(1,128)S(1)}, u32[]{:S(2)}) copy-start(s32[1,1,2,512]{3,0,2,1:T(1,128)S(1)} %copy.150) | copy-start | bytes 12292
  20.1 10.1 %copy-start.15 = (s32[1,1,2,512]{3,0,2,1:T(1,128)}, s32[1,1,2,512]{3,0,2,1:T(1,128)S(1)}, u32[]{:S(2)}) copy-start(s32[1,1,2,512]{3,0,2,1:T(1,128)S(1)} %copy.149) | copy-start | bytes 12292
  21.2 9.1 %copy-start.16 = (s32[1,1,2,512]{3,0,2,1:T(1,128)}, s32[1,1,2,512]{3,0,2,1:T(1,128)S(1)}, u32[]{:S(2)}) copy-start(s32[1,1,2,512]{3,0,2,1:T(1,128)S(1)} %copy.148) | copy-start | bytes 12292
  417.3 110.8 %copy-start.10 = (f32[8,768]{1,0:T(8,128)S(1)}, f32[8,768]{1,0:T(8,128)}, u32[]{:S(2)}) copy-start(f32[8,768]{1,0:T(8,128)} %get-tuple-element.75) | copy-start | bytes 73732
  528.1 3.5 copy-start.8
  528.1 3.8 copy-start.18
  528.1 3.8 copy-start.19
  533.2 162.4 %reduce-scatter.7.cloned.1.call-start = ((), (), s32[]{:S(2)}) async-start(), calls=%async_computation.9 | async-start | bytes 884736 | tf_op jit(solution)/shard_map/reduce_scatter | solution.py:673
  534.6 216.3 %reduce-scatter.5.cloned.1.call-start = ((), (), s32[]{:S(2)}) async-start(), calls=%async_computation.8 | async-start | bytes 2654208 | tf_op jit(solution)/shard_map/reduce_scatter | solution.py:673
  539.7 266.8 %reduce-scatter.11.cloned.1.call-start = ((), (), s32[]{:S(2)}) async-start(), calls=%async_computation.11 | async-start | bytes 2654208 | tf_op jit(solution)/shard_map/reduce_scatter | solution.py:673
  544.8 317.3 %reduce-scatter.9.cloned.1.call-start = ((), (), s32[]{:S(2)}) async-start(), calls=%async_computation.10 | async-start | bytes 2654208 | tf_op jit(solution)/shard_map/reduce_scatter | solution.py:673
  551.3 2.9 copy-start.1
  551.3 2.9 copy-start.7
  554.2 143.0 %collective-permute-start.1 = (bf16[2,512,768]{2,1,0:T(8,128)(2,1)}, bf16[2,512,768]{2,1,0:T(8,128)(2,1)}, u32[]{:S(2)}, u32[]{:S(2)}) collective-permute-start(bf16[2,512,768]{2,1,0:T(8,128)(2,1)} %get-tuple-element.135), channel_id=1, source_target_pairs={{0,16},{16,0},{1,17},{17,1},{2,18},{18,2},{3,19},{19,3},{4,20},{20... | collective-permute-start | bytes 4718600 | tf_op jit(solution)/shard_map/ppermute | solution.py:662
  555.5 146.0 %collective-permute-start = (bf16[2,512,768]{2,1,0:T(8,128)(2,1)}, bf16[2,512,768]{2,1,0:T(8,128)(2,1)}, u32[]{:S(2)}, u32[]{:S(2)}) collective-permute-start(bf16[2,512,768]{2,1,0:T(8,128)(2,1)} %get-tuple-element.137), channel_id=1, source_target_pairs={{0,16},{16,0},{1,17},{17,1},{2,18},{18,2},{3,19},{19,3},{4,20},{20... | collective-permute-start | bytes 4718600 | tf_op jit(solution)/shard_map/ppermute | solution.py:662
  (6 other events, 10.2 us)
Sparse Core Ops, SparseCore 0:
  9.6 12.8 all-gather.6
  24.1 12.0 all-gather.10
  37.7 12.1 all-gather.8
  533.3 124.2 all-reduce.1
  659.7 35.8 reduce-scatter.6
  697.8 53.0 reduce-scatter.4
  753.3 53.1 reduce-scatter.10
  809.0 53.1 reduce-scatter.8

commit v2 on v0

v2 whole, which is shorter than its diff:
```python
import functools

import jax
import jax.numpy as jnp
from jax import lax
from jax.experimental import pallas as pl
from jax.experimental.pallas import tpu as pltpu
from jax.sharding import PartitionSpec as P

HEAD_DIM = 64
CLUSTER = 128
ITEMS = 6
EPSILON = 1e-06
MESH = pl.DeviceIdType.MESH
VMEM_LIMIT = 60 * 1024 * 1024
bf16 = jnp.bfloat16
f32 = jnp.float32


def nn(a, b):
    return lax.dot_general(a, b, (((1,), (0,)), ((), ())), preferred_element_type=f32)


def nt(a, b):
    return lax.dot_general(a, b, (((1,), (1,)), ((), ())), preferred_element_type=f32)


def tn(a, b):
    return lax.dot_general(a, b, (((0,), (0,)), ((), ())), preferred_element_type=f32)


def loop(count, body):
    def step(index, carry):
        body(index)
        return carry

    lax.fori_loop(0, count, step, 0)


def rows_at(index, size):
    return pl.ds(pl.multiple_of(index * size, size), size)


class Bag:
    def __init__(self, names, values):
        self.__dict__.update(zip(names, values, strict=True))


def place_rows(row, first, count):
    numbers = lax.broadcasted_iota(jnp.int32, (count, row.shape[1]), 0) + first
    return (numbers == row).astype(bf16)


def by_head(block, heads):
    lane = lax.broadcasted_iota(jnp.int32, block.shape, 1) // HEAD_DIM
    return jnp.concatenate([jnp.where(lane == h, block, jnp.zeros_like(block)) for h in range(heads)])


def fold_heads(stacked, heads):
    count = stacked.shape[0] // heads
    lane = lax.broadcasted_iota(jnp.int32, (count, stacked.shape[1]), 1) // HEAD_DIM
    total = jnp.where(lane == 0, stacked[:count], 0.0)
    for h in range(1, heads):
        total = jnp.where(lane == h, stacked[h * count : (h + 1) * count], total)
    return total


def softmax_parts(scores, same):
    masked = jnp.where(same, scores, -1e30)
    centred = masked - jnp.max(masked, axis=-1, keepdims=True)
    grown = jnp.exp(centred)
    total = jnp.sum(grown, axis=-1, keepdims=True)
    return grown / total, centred, total


def same_item(row):
    wide = jnp.broadcast_to(row.astype(f32), (row.shape[1], row.shape[1]))
    return wide == wide.T


def normalise(values):
    centre = jnp.mean(values, axis=-1, keepdims=True)
    spread = values - centre
    second = jnp.mean(spread * spread, axis=-1, keepdims=True)
    inverse = lax.rsqrt(second + EPSILON)
    return spread * inverse, inverse


def norm_backward(grad, normed, inverse, gain):
    scaled = grad * gain
    first = jnp.mean(scaled, axis=-1, keepdims=True)
    second = jnp.mean(scaled * normed, axis=-1, keepdims=True)
    return inverse * (scaled - first - normed * second)


def column_sum(value):
    return jnp.sum(value.astype(f32), axis=0, keepdims=True)


def remote(src, dst, sems, device):
    return pltpu.make_async_remote_copy(
        src_ref=src, dst_ref=dst, send_sem=sems[0], recv_sem=sems[1],
        device_id=device, device_id_type=MESH,
    )


def layers_kernel(n_z, n_t, rows, width, cols, names, *refs):
    r = Bag(names, refs)
    heads, half_width = cols // HEAD_DIM, width // 2
    scale = HEAD_DIM**-0.5
    core, z, t = lax.axis_index("section"), lax.axis_index("dp"), lax.axis_index("tensor")
    other = {"section": 1 - core}
    step_x, step_y = 1 - 2 * lax.rem(t, 2), 2 - 4 * (t // 2)
    t_x, t_y = t + step_x, t + step_y
    t_far = t + step_x + step_y
    piece, own = rows // n_z, rows // n_t
    chunk_rows = max(piece, 128)
    chunks, per_chunk = rows // chunk_rows, chunk_rows // piece
    mine = rows_at(t, own)
    weights = ("wa", "wo", "wu", "wd")

    def load(i):
        if i < 2:
            return pltpu.make_async_copy(r.x_in.at[core * 2 + i], r.x.at[i], r.load_sem.at[i])
        if i < 4:
            return pltpu.make_async_copy(r.g_in.at[core * 2 + i - 2], r.g.at[i - 2], r.load_sem.at[i])
        name = weights[i - 4]
        return pltpu.make_async_copy(
            getattr(r, name + "_in"), getattr(r, name).at[core], r.load_sem.at[i]
        )

    def swap(i):
        sems = (r.swap_s.at[i], r.swap_r.at[i])
        if i == 4:
            return remote(r.idx_in, r.idx.at[core], sems, other)
        if i == 5:
            return remote(r.par_in, r.par.at[core], sems, other)
        name = weights[i]
        return remote(getattr(r, name + "_in"), getattr(r, name).at[core], sems, other)

    def start():
        for i in (0, 4, 1, 5, 6, 7, 2, 3):
            load(i).start()
        r.idx[core] = r.idx_in[...]
        r.par[core] = r.par_in[...]
        r.vec[...] = jnp.zeros(r.vec.shape, f32)
        barrier = pltpu.get_barrier_semaphore()
        pl.semaphore_signal(barrier, inc=1, device_id=other, device_id_type=MESH)

        def greet_z(k):
            peer = lax.rem(z + 1 + k, n_z)
            pl.semaphore_signal(barrier, inc=1, device_id={"dp": peer}, device_id_type=MESH)

        def greet_t(k):
            peer = lax.rem(t + 1 + k, n_t)
            pl.semaphore_signal(barrier, inc=1, device_id={"tensor": peer}, device_id_type=MESH)

        loop(n_z - 1, greet_z)
        loop(n_t - 1, greet_t)
        pl.semaphore_wait(barrier, n_z + n_t - 1)
        for i in (4, 5, 0, 1, 2, 3):
            swap(i).start()
        swap(4).wait()
        swap(5).wait()

    def need_weight(layer, i):
        @pl.when(core == layer)
        def _():
            load(4 + i).wait()

        @pl.when(core != layer)
        def _():
            swap(i).wait_recv()

    def index_cut(kind, layer, m, first, count):
        cuts = [
            r.idx[layer, kind * 4 + core * 2 + m, first // 128 + i] for i in range(count // 128)
        ]
        return cuts[0] if len(cuts) == 1 else jnp.concatenate(cuts, axis=1)

    def index_row(kind, layer, m):
        return index_cut(kind, layer, m, 0, rows)

    def par(layer, i, count=None):
        return r.par[layer, i : i + 1, : count or width]

    def z_copy(kind, m, k, src, dst):
        peer = lax.rem(z + k, n_z)
        return remote(
            src.at[rows_at(peer, piece)], dst.at[rows_at(z, piece)],
            (r.z_s.at[kind, m, k - 1], r.z_r.at[kind, m, k - 1]), {"dp": peer},
        )

    def z_chunk(kk):
        return lax.rem(z // per_chunk + 1 + kk, chunks)

    def z_send(kind, m, cc, src, dst):
        def one(j):
            peer = cc * per_chunk + j
            k = lax.rem(peer - z + n_z, n_z)

            @pl.when(k > 0)
            def _():
                z_copy(kind, m, k, src, dst).start()

        loop(per_chunk, one)

    def z_wait(kind, m, src, dst):
        loop(n_z - 1, lambda k: z_copy(kind, m, k + 1, src, dst).wait())

    def keep_piece(src, dst, m):
        here = rows_at(z, piece)
        dst[m, here] = src[m, here]

    left, right = slice(0, half_width), slice(half_width, width)

    def sum_copy(m, j):
        peer = t_x if j in (0, 1, 5) else t_y
        return remote(
            r.sum_src.at[m, j], r.sum_dst.at[m, j], (r.sum_s.at[m, j], r.sum_r.at[m, j]),
            {"tensor": peer},
        )

    def sum_put(m, role, part):
        @pl.when(role == 0)
        def _():
            r.sum_own[m] = part

        @pl.when(role == 1)
        def _():
            r.sum_src[m, 1] = part[:, left].astype(bf16)
            r.sum_keep[m, 1] = part[:, right]
            sum_copy(m, 1).start()

        @pl.when(role == 2)
        def _():
            r.sum_src[m, 3] = part[:, right].astype(bf16)
            r.sum_keep[m, 0] = part[:, left]
            sum_copy(m, 3).start()

        @pl.when(role == 3)
        def _():
            r.sum_src[m, 0] = part[:, left].astype(bf16)
            sum_copy(m, 0).start()
            r.sum_src[m, 2] = part[:, right].astype(bf16)
            sum_copy(m, 2).start()

    def sum_mid(m):
        sum_copy(m, 0).wait_recv()
        r.sum_src[m, 4] = (r.sum_keep[m, 0] + r.sum_dst[m, 0].astype(f32)).astype(bf16)
        sum_copy(m, 4).start()
        sum_copy(m, 2).wait_recv()
        r.sum_src[m, 5] = (r.sum_keep[m, 1] + r.sum_dst[m, 2].astype(f32)).astype(bf16)
        sum_copy(m, 5).start()

    def sum_take(m):
        for j in (1, 3, 4, 5):
            sum_copy(m, j).wait_recv()
        for j in range(6):
            sum_copy(m, j).wait_send()
        added = jnp.concatenate(
            [
                r.sum_dst[m, 1].astype(f32) + r.sum_dst[m, 4].astype(f32),
                r.sum_dst[m, 3].astype(f32) + r.sum_dst[m, 5].astype(f32),
            ],
            axis=1,
        )
        return r.sum_own[m] + added

    def role_rows(role):
        return rows_at(t + lax.rem(role, 2) * step_x + (role // 2) * step_y, own)

    def gather_copy(kind, m, j, buf):
        if j < 2:
            here = mine
        elif j == 2:
            here = pl.ds(pl.multiple_of(t_x * own, own), own // 2)
        else:
            here = pl.ds(pl.multiple_of(t_y * own + own // 2, own // 2), own // 2)
        return remote(
            buf.at[here], buf.at[here], (r.gather_s.at[kind, m, j], r.gather_r.at[kind, m, j]),
            {"tensor": t_x if j in (0, 3) else t_y},
        )

    def gather_start(kind, m, buf):
        gather_copy(kind, m, 0, buf).start()
        gather_copy(kind, m, 1, buf).start()

    def gather_on(kind, m, buf):
        gather_copy(kind, m, 0, buf).wait_recv()
        gather_copy(kind, m, 2, buf).start()
        gather_copy(kind, m, 1, buf).wait_recv()
        gather_copy(kind, m, 3, buf).start()

    def gather_far(kind, m, buf):
        gather_copy(kind, m, 2, buf).wait_recv()
        gather_copy(kind, m, 3, buf).wait_recv()

    def gather_sent(kind, m, buf):
        for j in range(4):
            gather_copy(kind, m, j, buf).wait_send()

    def gather_step(kind, m, role, buf):
        @pl.when(role == 1)
        def _():
            gather_on(kind, m, buf)

        @pl.when(role == 3)
        def _():
            gather_far(kind, m, buf)

    def out_local(kind, m, src, out):
        return pltpu.make_async_copy(src, out.at[core * 2 + m], r.out_l.at[kind, m])

    def out_away(kind, m, src, out):
        return remote(src, out.at[core * 2 + m], (r.out_s.at[kind, m], r.out_r.at[kind, m]), other)

    def out_start(kind, layer, m, src, out):
        @pl.when(core == layer)
        def _():
            out_local(kind, m, src, out).start()

        @pl.when(core != layer)
        def _():
            out_away(kind, m, src, out).start()

    def out_wait(kind, layer, m, src, out):
        @pl.when(core == layer)
        def _():
            out_local(kind, m, src, out).wait()

        @pl.when(core != layer)
        def _():
            out_away(kind, m, src, out).wait_send()

    def project(l, m):
        if m == 0:
            need_weight(l, 0)
        if l == 0:
            load(m).wait()

        def chunk(kk):
            cc = z_chunk(kk)
            here = rows_at(cc, chunk_rows)
            numbers = lax.broadcasted_iota(jnp.int32, (rows, chunk_rows), 0)
            pick = (numbers == index_cut(1, l, m, cc * chunk_rows, chunk_rows)).astype(bf16)
            moved = tn(pick, r.x[m]).astype(bf16)
            r.xp[l, m, here] = moved
            r.zs[m, here] = (nn(moved, r.wa[l]) + par(l, 0, 3 * cols)).astype(bf16)
            z_send(0, m, cc, r.zs.at[m], r.zr.at[m])

        loop(chunks, chunk)
        keep_piece(r.zs, r.zr, m)

    def attend(l, m):
        z_wait(0, m, r.zs.at[m], r.zr.at[m])
        lane = lax.broadcasted_iota(jnp.int32, (1, 128), 1)

        def cluster(c):
            here = rows_at(c, CLUSTER)
            numbers = lax.broadcasted_iota(jnp.int32, (rows, CLUSTER), 0)
            pick = (numbers == index_cut(2, l, m, c * CLUSTER, CLUSTER)).astype(bf16)
            block = tn(pick, r.zr[m]).astype(bf16)
            r.grouped[l, m, here] = block
            queries, keys, values = (block[:, i * cols : (i + 1) * cols] for i in range(3))
            scores = nt(queries, by_head(keys, heads)) * scale
            same = same_item(index_cut(0, l, m, c * CLUSTER, CLUSTER))
            probs = []
            log_row = jnp.zeros((1, 128), f32)
            for h in range(heads):
                cut = slice(h * CLUSTER, (h + 1) * CLUSTER)
                prob, centred, total = softmax_parts(scores[:, cut], same)
                inner = jnp.sum(jnp.where(same, prob * centred, 0.0), axis=-1, keepdims=True)
                entropy = jnp.mean(jnp.log(total) - inner, axis=0, keepdims=True)
                log_row = jnp.where(lane == h, entropy, log_row)
                probs.append(prob.astype(bf16))
            r.entropy[l, m, pl.ds(c, 1)] = log_row
            mixed = nn(jnp.concatenate(probs, axis=1), by_head(values, heads))
            r.mixc[m, here] = mixed.astype(bf16)

        loop(rows // CLUSTER, cluster)

        def home(kk):
            cc = z_chunk(kk)
            here = rows_at(cc, chunk_rows)
            one_hot = place_rows(index_row(2, l, m), cc * chunk_rows, chunk_rows)
            r.ms_src[m, here] = nn(one_hot, r.mixc[m]).astype(bf16)
            z_send(1, m, cc, r.ms_src.at[m], r.ms.at[l, m])

        loop(chunks, home)
        here = rows_at(z, piece)
        r.ms[l, m, here] = r.ms_src[m, here]

    def out_project(l, m):
        if m == 0:
            need_weight(l, 1)
        z_wait(1, m, r.ms_src.at[m], r.ms.at[l, m])

        def part(kk):
            role = 3 - kk
            sum_put(m, role, nn(r.ms[l, m, role_rows(role)], r.wo[l]))

        loop(n_t, part)

    def middle(l, m):
        sum_mid(m)

    def first_norm(l, m):
        total = sum_take(m) + par(l, 1)
        normed, inverse = normalise(r.xp[l, m, mine].astype(f32) + total)
        hidden = normed * par(l, 2) + par(l, 3)
        r.n1[l, m] = normed
        r.inv1[l, m] = jnp.broadcast_to(inverse, (own, 128))
        r.hid[m] = hidden
        r.hfull[l, m, mine] = hidden.astype(bf16)
        gather_start(0, m, r.hfull.at[l, m])

    def feed(l, m):
        if m == 0:
            need_weight(l, 2)
            need_weight(l, 3)

        def part(role):
            gather_step(0, m, role, r.hfull.at[l, m])
            here = role_rows(role)
            up = nn(r.hfull[l, m, here], r.wu[l]) + par(l, 4)
            square = up * up
            tanh = jnp.tanh(0.7978845608028654 * up * (1.0 + 0.044715 * square))
            half = 0.5 * (1.0 + tanh)
            slope = 0.7978845608028654 * (1.0 + 3 * 0.044715 * square)
            r.gp[l, m, here] = (half + 0.5 * up * (1.0 - tanh * tanh) * slope).astype(bf16)
            active = (up * half).astype(bf16)
            r.act[l, m, here] = active
            sum_put(m, role, nn(active, r.wd[l]))

        loop(n_t, part)

    def second_norm(l, m):
        gather_sent(0, m, r.hfull.at[l, m])
        total = sum_take(m) + par(l, 5)
        normed, inverse = normalise(r.hid[m] + total)
        r.n2[l, m] = normed
        r.inv2[l, m] = jnp.broadcast_to(inverse, (own, 128))
        r.ag[m, mine] = (normed * par(l, 6) + par(l, 7)).astype(bf16)
        gather_start(1, m, r.ag.at[m])

    def out_on(l, m):
        gather_on(1, m, r.ag.at[m])

    def to_tokens(l, m, dst, buf):
        def chunk(cc):
            one_hot = place_rows(index_row(1, l, m), cc * 128, 128)
            dst[m, rows_at(cc, 128)] = nn(one_hot, buf[m]).astype(bf16)

        loop(rows // 128, chunk)

    def out_tokens(l, m):
        gather_far(1, m, r.ag.at[m])
        gather_sent(1, m, r.ag.at[m])
        if l == 1:
            out_wait(0, 0, m, r.x.at[m], r.acts)
        to_tokens(l, m, r.x, r.ag)
        out_start(0, l, m, r.x.at[m], r.acts)

    def add_vec(l, index, value):
        r.vec[l, index : index + 1, : value.shape[1]] += value

    def b_second_norm(l, m):
        if l == 1:
            load(2 + m).wait()
        numbers = lax.broadcasted_iota(jnp.int32, (rows, own), 0)
        pick = (numbers == index_cut(1, l, m, t * own, own)).astype(bf16)
        up = tn(pick, r.g[m])
        normed = r.n2[l, m]
        down = norm_backward(up, normed, r.inv2[l, m][:, :1], par(l, 6))
        r.hid[m] = down
        low = down.astype(bf16)
        r.db[m, mine] = low
        gather_start(2, m, r.db.at[m])
        add_vec(l, 0, column_sum(up * normed))
        add_vec(l, 1, column_sum(up))
        add_vec(l, 2, column_sum(low))

    def b_feed(l, m):
        def part(role):
            gather_step(2, m, role, r.db.at[m])
            here = role_rows(role)
            low = (nt(r.db[m, here], r.wd[l]) * r.gp[l, m, here].astype(f32)).astype(bf16)
            r.gp[l, m, here] = low
            sum_put(m, role, nt(low, r.wu[l]))

        loop(n_t, part)

    def grad_slabs(ref, value, lanes):
        ref[:, :, lanes] = value.reshape(n_z, width // n_z, value.shape[1]).astype(bf16)

    def feed_weights(l, m):
        for i in range(2):
            gather_sent(2, i, r.db.at[i])
            add_vec(l, 6, column_sum(r.gp[l, i]))
        up = tn(r.hfull[l, 0], r.gp[l, 0]) + tn(r.hfull[l, 1], r.gp[l, 1])
        grad_slabs(r.gs_feed, up, slice(0, width))
        down = tn(r.db[0], r.act[l, 0]) + tn(r.db[1], r.act[l, 1])
        grad_slabs(r.gs_feed, down, slice(width, 2 * width))
        grads_send(0, l, r.gs_feed, r.gr_feed)

    def b_first_norm(l, m):
        up = r.hid[m] + sum_take(m)
        normed = r.n1[l, m]
        down = norm_backward(up, normed, r.inv1[l, m][:, :1], par(l, 2))
        r.dres[m] = down
        low = down.astype(bf16)
        r.da[m, mine] = low
        gather_start(3, m, r.da.at[m])
        add_vec(l, 3, column_sum(up * normed))
        add_vec(l, 4, column_sum(up))
        add_vec(l, 5, column_sum(low))

    def b_on(l, m):
        gather_on(3, m, r.da.at[m])

    def out_back(l, m):
        gather_far(3, m, r.da.at[m])
        gather_sent(3, m, r.da.at[m])

        def chunk(kk):
            cc = z_chunk(kk)
            here = rows_at(cc, chunk_rows)
            r.ms_src[m, here] = nt(r.da[m, here], r.wo[l]).astype(bf16)
            z_send(2, m, cc, r.ms_src.at[m], r.dmr.at[m])

        loop(chunks, chunk)
        keep_piece(r.ms_src, r.dmr, m)

    def out_weights(l, m):
        value = tn(r.da[0], r.ms[l, 0]) + tn(r.da[1], r.ms[l, 1])
        grad_slabs(r.gs_attn, value, slice(3 * cols, 4 * cols))

    def b_attend(l, m):
        z_wait(2, m, r.ms_src.at[m], r.dmr.at[m])

        def cluster(c):
            here = rows_at(c, CLUSTER)
            numbers = lax.broadcasted_iota(jnp.int32, (rows, CLUSTER), 0)
            pick = (numbers == index_cut(2, l, m, c * CLUSTER, CLUSTER)).astype(bf16)
            dmix = tn(pick, r.dmr[m]).astype(bf16)
            block = r.grouped[l, m, here]
            queries, keys, values = (block[:, i * cols : (i + 1) * cols] for i in range(3))
            keys_by_head = by_head(keys, heads)
            scores = nt(queries, keys_by_head) * scale
            same = same_item(index_cut(0, l, m, c * CLUSTER, CLUSTER))
            dprob = nt(dmix, by_head(values, heads))
            probs, dscores = [], []
            for h in range(heads):
                cut = slice(h * CLUSTER, (h + 1) * CLUSTER)
                prob = softmax_parts(scores[:, cut], same)[0]
                outer = prob * dprob[:, cut]
                dscore = outer - prob * jnp.sum(outer, axis=-1, keepdims=True)
                probs.append(prob.astype(bf16))
                dscores.append(dscore.astype(bf16))
            prob_all = jnp.concatenate(probs, axis=1)
            dscore_all = jnp.concatenate(dscores, axis=1)
            dqueries = nn(dscore_all, keys_by_head) * scale
            dkeys = fold_heads(tn(dscore_all, queries), heads) * scale
            dvalues = fold_heads(tn(prob_all, dmix), heads)
            r.grouped[l, m, here] = jnp.concatenate([dqueries, dkeys, dvalues], axis=1).astype(bf16)

        loop(rows // CLUSTER, cluster)

        def home(kk):
            cc = z_chunk(kk)
            here = rows_at(cc, chunk_rows)
            one_hot = place_rows(index_row(2, l, m), cc * chunk_rows, chunk_rows)
            r.zs[m, here] = nn(one_hot, r.grouped[l, m]).astype(bf16)
            z_send(3, m, cc, r.zs.at[m], r.zr.at[m])

        loop(chunks, home)
        keep_piece(r.zs, r.zr, m)

    def in_project(l, m):
        z_wait(3, m, r.zs.at[m], r.zr.at[m])

        def part(kk):
            role = 3 - kk
            sum_put(m, role, nt(r.zr[m, role_rows(role)], r.wa[l]))

        loop(n_t, part)

    def in_weights(l, m):
        for i in range(2):
            add_vec(l, 7, column_sum(r.zr[i]))
        value = tn(r.xp[l, 0], r.zr[0]) + tn(r.xp[l, 1], r.zr[1])
        grad_slabs(r.gs_attn, value, slice(0, 3 * cols))
        grads_send(1, l, r.gs_attn, r.gr_attn)

    def layer_input(l, m):
        r.ag[m, mine] = (r.dres[m] + sum_take(m)).astype(bf16)
        gather_start(4, m, r.ag.at[m])

    def b_out_on(l, m):
        gather_on(4, m, r.ag.at[m])

    def b_tokens(l, m):
        gather_far(4, m, r.ag.at[m])
        gather_sent(4, m, r.ag.at[m])
        if l == 0:
            out_wait(1, 1, m, r.g.at[m], r.grads)
        to_tokens(l, m, r.g, r.ag)
        out_start(1, l, m, r.g.at[m], r.grads)

    def grad_core_copy(kind, k, src, dst):
        return remote(src.at[k], dst.at[k], (r.gc_s.at[kind, k], r.gc_r.at[kind, k]), other)

    def grad_z_copy(kind, k, src, dst):
        peer = lax.rem(z + k, n_z)
        return remote(
            src.at[peer], dst.at[k - 1], (r.gz_s.at[kind, k - 1], r.gz_r.at[kind, k - 1]),
            {"dp": peer},
        )

    def grads_send(kind, l, src, dst):
        @pl.when(core != l)
        def _():
            loop(n_z, lambda k: grad_core_copy(kind, lax.rem(z + 1 + k, n_z), src, dst).start())

    def grads_mid(kind, l, src, came, dst):
        @pl.when(core == l)
        def _():
            def one(kk):
                k = lax.rem(kk + 1, n_z)
                peer = lax.rem(z + k, n_z)
                grad_core_copy(kind, peer, src, came).wait_recv()
                src[peer] = (src[peer].astype(f32) + came[peer].astype(f32)).astype(bf16)

                @pl.when(k > 0)
                def _():
                    grad_z_copy(kind, k, src, dst).start()

            loop(n_z, one)

    def grads_end(kind, l, src, came, dst, out):
        @pl.when(core == l)
        def _():
            out[...] = src[z].astype(f32)

            def one(k):
                grad_z_copy(kind, k + 1, src, dst).wait()
                out[...] += dst[k].astype(f32)

            loop(n_z - 1, one)

        @pl.when(core != l)
        def _():
            loop(n_z, lambda k: grad_core_copy(kind, k, src, came).wait_send())

    def feed_mid(l, m):
        grads_mid(0, l, r.gs_feed, r.gr_feed, r.gz_feed)

    def feed_end(l, m):
        grads_end(0, l, r.gs_feed, r.gr_feed, r.gz_feed, r.g_feed)

    def attn_mid(l, m):
        grads_mid(1, l, r.gs_attn, r.gr_attn, r.gz_attn)

    def attn_end(l, m):
        grads_end(1, l, r.gs_attn, r.gr_attn, r.gz_attn, r.g_attn)

    def vec_copy(l):
        return remote(r.vec.at[l], r.vec_came, (r.vc_s.at[0], r.vc_r.at[0]), other)

    def vec_t_copy(k):
        return remote(
            r.vec_t.at[t], r.vec_t.at[t], (r.vt_s.at[k - 1], r.vt_r.at[k - 1]),
            {"tensor": lax.rem(t + k, n_t)},
        )

    def vec_z_copy(k):
        return remote(
            r.vec_z.at[z], r.vec_z.at[z], (r.vz_s.at[k - 1], r.vz_r.at[k - 1]),
            {"dp": lax.rem(z + k, n_z)},
        )

    def entropy_copy(l, m):
        return remote(
            r.entropy.at[l, m], r.ent.at[core * 2 + m], (r.en_s.at[m], r.en_r.at[m]), other
        )

    def vec_start(l, m):
        @pl.when(core != l)
        def _():
            vec_copy(l).start()
            for i in range(2):
                entropy_copy(l, i).start()

    def vec_sum_t(l, m):
        @pl.when(core == l)
        def _():
            for i in range(2):
                r.ent[core * 2 + i] = r.entropy[l, i]
            vec_copy(l).wait_recv()
            r.vec_t[t] = r.vec[l] + r.vec_came[...]
            for k in range(1, n_t):
                vec_t_copy(k).start()

    def vec_sum_z(l, m):
        @pl.when(core == l)
        def _():
            for k in range(1, n_t):
                vec_t_copy(k).wait()
            total = r.vec_t[0]
            for k in range(1, n_t):
                total = total + r.vec_t[k]
            lane_rows = lax.broadcasted_iota(jnp.int32, total.shape, 0)
            r.vec_z[z] = jnp.where(lane_rows < 6, total, r.vec_t[t])
            loop(n_z - 1, lambda k: vec_z_copy(k + 1).start())

    def vec_end(l, m):
        @pl.when(core == l)
        def _():
            loop(n_z - 1, lambda k: vec_z_copy(k + 1).wait())
            r.vec_out[...] = r.vec_z[0]

            def one(k):
                r.vec_out[...] += r.vec_z[k + 1]

            loop(n_z - 1, one)

        @pl.when(core != l)
        def _():
            vec_copy(l).wait_send()
            for i in range(2):
                entropy_copy(l, i).wait_send()

    def finish():
        for m in range(2):
            out_wait(0, 1, m, r.x.at[m], r.acts)
            out_wait(1, 0, m, r.g.at[m], r.grads)
            for kind, out, src in ((0, r.acts, r.x), (1, r.grads, r.g)):
                out_away(kind, m, src.at[m], out).wait_recv()
            entropy_copy(0, m).wait_recv()
        for i in range(4):
            swap(i).wait_send()

    schedule = (
        (project, 0, 0), (attend, 0, 0), (project, 0, 1), (out_project, 0, 0), (middle, 0, 0),
        (first_norm, 0, 0), (attend, 0, 1), (feed, 0, 0), (middle, 0, 0), (out_project, 0, 1),
        (second_norm, 0, 0), (middle, 0, 1), (out_on, 0, 0), (first_norm, 0, 1), (out_tokens, 0, 0),
        (project, 1, 0), (feed, 0, 1), (middle, 0, 1), (attend, 1, 0), (second_norm, 0, 1), (out_on, 0, 1),
        (out_project, 1, 0), (out_tokens, 0, 1), (project, 1, 1), (middle, 1, 0), (first_norm, 1, 0),
        (attend, 1, 1), (feed, 1, 0), (middle, 1, 0), (out_project, 1, 1), (second_norm, 1, 0),
        (middle, 1, 1), (b_second_norm, 1, 0), (out_on, 1, 0), (first_norm, 1, 1), (out_tokens, 1, 0),
        (b_feed, 1, 0), (feed, 1, 1), (middle, 1, 0), (middle, 1, 1), (b_first_norm, 1, 0),
        (second_norm, 1, 1), (b_on, 1, 0), (b_second_norm, 1, 1), (out_on, 1, 1), (out_back, 1, 0),
        (out_tokens, 1, 1), (b_feed, 1, 1), (middle, 1, 1), (b_attend, 1, 0), (b_first_norm, 1, 1),
        (feed_weights, 1, 1), (b_on, 1, 1), (in_project, 1, 0), (feed_mid, 1, 0), (out_back, 1, 1),
        (middle, 1, 0), (layer_input, 1, 0), (out_weights, 1, 1), (b_out_on, 1, 0), (b_attend, 1, 1),
        (b_tokens, 1, 0), (b_second_norm, 0, 0), (in_project, 1, 1), (b_feed, 0, 0), (middle, 1, 1),
        (middle, 0, 0), (in_weights, 1, 1), (vec_start, 1, 0), (layer_input, 1, 1), (b_first_norm, 0, 0),
        (b_out_on, 1, 1), (b_on, 0, 0), (b_tokens, 1, 1), (out_back, 0, 0), (b_second_norm, 0, 1),
        (attn_mid, 1, 0), (vec_sum_t, 1, 0), (b_feed, 0, 1), (middle, 0, 1), (b_attend, 0, 0),
        (feed_end, 1, 0), (b_first_norm, 0, 1), (vec_sum_z, 1, 0), (feed_weights, 0, 1), (b_on, 0, 1),
        (in_project, 0, 0), (out_back, 0, 1), (middle, 0, 0), (feed_mid, 0, 0), (layer_input, 0, 0),
        (vec_end, 1, 0), (attn_end, 1, 0), (out_weights, 0, 1), (b_attend, 0, 1), (b_out_on, 0, 0),
        (b_tokens, 0, 0), (in_project, 0, 1), (in_weights, 0, 1), (attn_mid, 0, 0), (middle, 0, 1),
        (vec_start, 0, 0), (layer_input, 0, 1), (vec_sum_t, 0, 0), (b_out_on, 0, 1), (vec_sum_z, 0, 0),
        (b_tokens, 0, 1), (feed_end, 0, 0), (vec_end, 0, 0), (attn_end, 0, 0),
    )
    start()
    for step, layer, micro in schedule:
        step(layer, micro)
    finish()


def run_layers(n_z, x, g, idx, par, wa, wo, wu, wd):
    micros, rows, width = x.shape
    cols, hidden = wo.shape[0], wu.shape[1]
    n_t = lax.axis_size("tensor")
    own, slab = rows // n_t, width // n_z
    pair = (2, rows)
    both = (2, 2, rows)
    anywhere, vmem = pl.BlockSpec(memory_space=pl.ANY), pl.BlockSpec(memory_space=pltpu.VMEM)
    ins = dict(
        x_in=anywhere, g_in=anywhere, idx_in=vmem, par_in=vmem, wa_in=anywhere, wo_in=anywhere,
        wu_in=anywhere, wd_in=anywhere,
    )
    outs = dict(
        acts=(anywhere, x.shape, bf16), grads=(anywhere, x.shape, bf16),
        g_feed=(vmem, (slab, 2 * width), f32), g_attn=(vmem, (slab, width), f32),
        vec_out=(vmem, (8, width), f32), ent=(vmem, (micros, max(8, rows // CLUSTER), 128), f32),
    )
    sem = pltpu.SemaphoreType.DMA
    scratch = dict(
        x=((*pair, width), bf16), g=((*pair, width), bf16),
        wa=((2, width, 3 * cols), bf16), wo=((2, cols, width), bf16),
        wu=((2, width, hidden), bf16), wd=((2, hidden, width), bf16),
        idx=((2, *idx.shape), jnp.int32), par=((2, *par.shape), f32),
        xp=((*both, width), bf16), grouped=((*both, 3 * cols), bf16), ms=((*both, cols), bf16),
        n1=((2, 2, own, width), f32), inv1=((2, 2, own, 128), f32), hfull=((*both, width), bf16),
        act=((*both, hidden), bf16), gp=((*both, hidden), bf16),
        n2=((2, 2, own, width), f32), inv2=((2, 2, own, 128), f32),
        entropy=((2, 2, max(8, rows // CLUSTER), 128), f32),
        zs=((*pair, 3 * cols), bf16), zr=((*pair, 3 * cols), bf16), mixc=((*pair, cols), bf16),
        ms_src=((*pair, cols), bf16), dmr=((*pair, cols), bf16),
        sum_src=((2, 6, own, width // 2), bf16), sum_dst=((2, 6, own, width // 2), bf16),
        sum_keep=((2, 2, own, width // 2), f32), sum_own=((2, own, width), f32),
        hid=((2, own, width), f32), dres=((2, own, width), f32),
        ag=((*pair, width), bf16), db=((*pair, width), bf16), da=((*pair, width), bf16),
        gs_feed=((n_z, slab, 2 * width), bf16), gr_feed=((n_z, slab, 2 * width), bf16),
        gz_feed=((n_z - 1, slab, 2 * width), bf16),
        gs_attn=((n_z, slab, width), bf16), gr_attn=((n_z, slab, width), bf16),
        gz_attn=((n_z - 1, slab, width), bf16),
        vec=((2, 8, width), f32), vec_came=((8, width), f32), vec_t=((n_t, 8, width), f32),
        vec_z=((n_z, 8, width), f32),
    )
    sems = dict(load_sem=(8,))
    for name, shape in dict(
        swap=(6,), z=(4, 2, n_z - 1), sum=(2, 6), gather=(5, 2, 4), out=(2, 2), gc=(2, n_z),
        gz=(2, n_z - 1), vc=(1,), vt=(n_t - 1,), vz=(n_z - 1,), en=(2,),
    ).items():
        sems[name + "_s"] = shape
        sems[name + "_r"] = shape
    sems["out_l"] = (2, 2)
    names = [*ins, *outs, *scratch, *sems]
    return pl.pallas_call(
        functools.partial(layers_kernel, n_z, n_t, rows, width, cols, names),
        out_shape=[jax.ShapeDtypeStruct(shape, dtype) for _, shape, dtype in outs.values()],
        in_specs=list(ins.values()),
        out_specs=[spec for spec, _, _ in outs.values()],
        scratch_shapes=[
            *(pltpu.VMEM(shape, dtype) for shape, dtype in scratch.values()),
            *(sem(shape) for shape in sems.values()),
        ],
        compiler_params=pltpu.CompilerParams(
            collective_id=0, has_side_effects=True, vmem_limit_bytes=VMEM_LIMIT
        ),
        name="layers",
    )(x, g, idx, par, wa, wo, wu, wd)


def shards(
    inputs, out_grad, items, send_order, recv_order,
    attn_weight, qv_bias, out_weight, out_bias, norm_first,
    up_weight, up_bias, down_weight, down_bias, norm_second,
):
    micros, rows, width = inputs.shape
    n_z = lax.axis_size("dp")
    cols = attn_weight.shape[3]
    heads = cols // HEAD_DIM
    clusters = rows // CLUSTER

    idx = jnp.concatenate(
        [items[0], send_order[0, :, 0], recv_order[0, :, 0], jnp.zeros((4, rows), jnp.int32)]
    ).reshape(16, rows // 128, 1, 128)
    ba = jnp.concatenate(
        [qv_bias[0, 0], jnp.zeros((cols,), f32), qv_bias[0, 1], jnp.zeros((width - 3 * cols,), f32)]
    )
    par = jnp.concatenate(
        [ba[None], out_bias, norm_first[0], up_bias, down_bias, norm_second[0]]
    )
    acts, grads, g_feed, g_attn, vec, ent = run_layers(
        n_z, inputs, out_grad, idx, par, attn_weight[0].reshape(width, 3 * cols), out_weight[0],
        up_weight[0], down_weight[0],
    )
    item_numbers = jnp.arange(ITEMS, dtype=jnp.int32)
    grid = items[0].reshape(micros, clusters, CLUSTER)
    occupancy = jnp.sum((grid[..., None] == item_numbers).astype(f32), axis=2)
    results = (
        acts, grads.astype(f32), ent[:, :clusters, :heads], occupancy,
        g_attn[:, : 3 * cols].reshape(-1, 3, cols),
        jnp.stack([vec[7, :cols], vec[7, 2 * cols : 3 * cols]]), g_attn[:, 3 * cols :].T,
        vec[5], vec[3:5], g_feed[:, :width], vec[6], g_feed[:, width:].T, vec[2], vec[0:2],
    )
    return tuple(value[None] for value in results)


def solution(mesh):
    return jax.shard_map(
        shards,
        mesh=mesh,
        in_specs=(
            P(None, "dp", None),
            P(None, "dp", None),
            P("section", None, "dp"),
            P("section", None, "dp", None),
            P("section", None, "dp", None),
            P("section", None, None, "tensor"),
            P("section", None, "tensor"),
            P("section", "tensor", None),
            P("section", None),
            P("section", None, None),
            P("section", None, "tensor"),
            P("section", "tensor"),
            P("section", "tensor", None),
            P("section", None),
            P("section", None, None),
        ),
        out_specs=(
            P("section", None, "dp", None),
            P("section", None, "dp", None),
            P("section", None, "dp", "tensor"),
            P("section", None, "dp", None),
            P("section", "dp", None, "tensor"),
            P("section", None, "tensor"),
            P("section", "tensor", "dp"),
            P("section", None),
            P("section", None, None),
            P("section", "dp", "tensor"),
            P("section", "tensor"),
            P("section", "tensor", "dp"),
            P("section", None),
            P("section", None, None),
        ),
        check_vma=False,
    )
```

time: 2500 us -> 435 us (0.17)
  waiting for transfers between devices: 1100 us -> 0 us
  local copies, waits for them, and re-layouts: 666 us -> 19.8 us
  Pallas kernels: 0 us -> 401 us
  other arithmetic: 374 us -> 7.33 us
  matrix products: 201 us -> 0 us
  starting transfers between devices: 107 us -> 0 us
    psum x20 -> x0, waiting for transfers between devices: 876 us -> none  [the longest x5 303 us: shards(): lax.psum(jnp.dot(active, w_down, preferred_element_type=jnp.float32), 'te...]
    pallas_call x0 -> x1, Pallas kernels: none -> 401 us  [run_layers(): pl.pallas_call(functools.partial(layers_kernel, n_z, n_t, rows, width, co...]
    unnamed x848 -> x11, local copies, waits for them, and re-layouts: 214 us -> 4.61 us
    all_to_all x20 -> x0, waiting for transfers between devices: 197 us -> none  [the longest x5 61.2 us: shards(): lax.all_to_all(jnp.concatenate([proj_sent, d_sent], axis=1), 'dp', split_...]
    dot_general x85 -> x0, matrix products: 181 us -> none  [the longest x5 25.4 us: shards(): jnp.einsum('td,tf->df', hidden.astype(jnp.bfloat16), d_up, preferred_elem...]
    gather x45 -> x0, local copies, waits for them, and re-layouts: 173 us -> none  [the longest x5 25.2 us: shards(): jnp.take(returned, send_back, axis=0)]
    reduce_sum x83 -> x1, other arithmetic: 161 us -> 0.1 us  [shards(): occupancy = jnp.sum((grid[..., None] == item_numbers).astype(f32), axis=2)]
    select_n x73 -> x0, other arithmetic: 134 us -> none  [the longest x8 17.4 us: shards(): jnp.take(grad_cl.reshape(row_count, 3, heads_here, HEAD_DIM), recv_back,...]
  transfers between devices with their start and end apart: 52 -> 0, of which waited for: 45 -> 0; matrix products, arithmetic and copies ran while one was open for 17% -> 0% of each run, Pallas kernels for 0% -> 0%
where the time goes in v2:
time: 435 us; the launch traced here: 429 us
  Pallas kernels  401 us (92%)
  local copies, waits for them, and re-layouts  19.8 us (5%)
  other arithmetic  7.33 us (2%)
    pallas_call x1, Pallas kernels, run_layers(): pl.pallas_call(functools.partial(layers_kernel, n_z, n_t, rows, width, co...  401 us

profile of v2, /device:TPU:0, one launch (start us, length us, event | category | flops | bytes accessed | tf_op | source)
XLA Modules:
  0.0 428.6 jit_solution(5763861300064111630)
XLA Ops:
  0.6 0.7 concatenate.16
  1.4 0.1 pad.9.clone
  1.4 1.4 add_add_fusion.refs_2_
  2.9 0.8 fusion.2
  3.6 0.1 pad_maximum_fusion
  3.7 1.4 concatenate.21.refs_3_
  5.1 2.2 copy.38.refs_4_
  7.3 400.6 %layers.1 = (bf16[4,512,768]{2,1,0:T(8,128)(2,1)}, bf16[4,512,768]{2,1,0:T(8,128)(2,1)}, f32[192,1536]{1,0:T(8,128)}, f32[192,768]{1,0:T(8,128)}, f32[8,768]{1,0:T(8,128)}, /*index=5*/f32[4,8,128]{2,1,0:T(8,128)}) custom-call(bf16[4,512,768]{2,1,0:T(8,128)(2,1)} %refs_0_.1, bf16[4,512,768]{2,1,0:T(8,128)(2,1)} %refs_1_.1, ...), custom_call_target="tpu_custom_call" | custom-call | tf_op jit(solution)/shard_map/layers/pallas_call | solution.py:824
  407.9 0.0 copy-start.3
  407.9 0.0 copy-start.1
  407.9 5.1 %bitcast_convert_fusion = f32[1,4,512,768]{3,2,1,0:T(8,128)} fusion(bf16[4,512,768]{2,1,0:T(8,128)(2,1)} %get-tuple-element.21), kind=kLoop, calls=%fused_computation | loop fusion | flops 1572864 | bytes 9437184 | tf_op jit(solution)/shard_map/broadcast_in_dim | solution.py:873
  413.1 0.0 copy-start.2
  413.1 0.0 copy-done.3
  413.1 0.7 copy.39
  413.8 0.0 copy-done.1
  413.8 0.1 convert_reduce_fusion
  413.9 0.7 copy.40
  414.6 0.0 copy-start
  414.6 2.0 slice.45
  416.6 2.1 copy.41
  418.7 2.1 copy.42
  420.8 0.0 copy-done.2
  420.8 0.6 maximum_bitcast_fusion
  421.4 1.0 slice_bitcast_fusion.2
  422.4 0.8 copy.43
  423.2 0.6 fusion
  423.8 0.6 slice_bitcast_fusion.3
  424.4 2.3 slice_bitcast_fusion
  426.7 0.0 copy-done
  426.7 1.7 copy.45
  (6 shorter events, 0.0 us)
Async XLA Ops:
  407.9 5.2 %copy-start.3 = (f32[4,8,128]{2,1,0:T(8,128)S(1)}, f32[4,8,128]{2,1,0:T(8,128)}, u32[]{:S(2)}) copy-start(f32[4,8,128]{2,1,0:T(8,128)} %get-tuple-element.22) | copy-start | bytes 49156
  407.9 5.9 %copy-start.1 = (s32[1,4,512]{2,1,0:T(4,128)S(1)}, s32[1,4,512]{2,1,0:T(4,128)}, u32[]{:S(2)}) copy-start(s32[1,4,512]{2,1,0:T(4,128)} %param.17) | copy-start | bytes 24580
  413.1 7.7 %copy-start.2 = (f32[8,768]{1,0:T(8,128)S(1)}, f32[8,768]{1,0:T(8,128)}, u32[]{:S(2)}) copy-start(f32[8,768]{1,0:T(8,128)} %get-tuple-element.24) | copy-start | bytes 73732
  414.6 12.1 %copy-start = (bf16[4,512,768]{2,1,0:T(8,128)(2,1)S(1)}, bf16[4,512,768]{2,1,0:T(8,128)(2,1)}, u32[]{:S(2)}) copy-start(bf16[4,512,768]{2,1,0:T(8,128)(2,1)} %get-tuple-element.20) | copy-start | bytes 9437188

commit v3 on v2

--- a/solution.py
+++ b/solution.py
@@ -12,7 +12,7 @@
 ITEMS = 6
 EPSILON = 1e-06
 MESH = pl.DeviceIdType.MESH
-VMEM_LIMIT = 60 * 1024 * 1024
+VMEM_LIMIT = 61 * 1024 * 1024
 bf16 = jnp.bfloat16
 f32 = jnp.float32
 
@@ -124,6 +124,8 @@
             return pltpu.make_async_copy(r.x_in.at[core * 2 + i], r.x.at[i], r.load_sem.at[i])
         if i < 4:
             return pltpu.make_async_copy(r.g_in.at[core * 2 + i - 2], r.g.at[i - 2], r.load_sem.at[i])
+        if i == 5:
+            return pltpu.make_async_copy(r.wo_in, r.wo.at[core, t], r.load_sem.at[i])
         name = weights[i - 4]
         return pltpu.make_async_copy(
             getattr(r, name + "_in"), getattr(r, name).at[core], r.load_sem.at[i]
@@ -132,17 +134,28 @@
     def swap(i):
         sems = (r.swap_s.at[i], r.swap_r.at[i])
         if i == 4:
-            return remote(r.idx_in, r.idx.at[core], sems, other)
+            return remote(r.idx.at[core], r.idx.at[core], sems, other)
         if i == 5:
-            return remote(r.par_in, r.par.at[core], sems, other)
+            return remote(r.par.at[core], r.par.at[core], sems, other)
+        if i == 1:
+            return remote(r.wo_in, r.wo.at[core, t], sems, other)
         name = weights[i]
         return remote(getattr(r, name + "_in"), getattr(r, name).at[core], sems, other)
 
     def start():
         for i in (0, 4, 1, 5, 6, 7, 2, 3):
             load(i).start()
-        r.idx[core] = r.idx_in[...]
-        r.par[core] = r.par_in[...]
+        for kind, index in enumerate((r.items_in, r.send_in, r.recv_in)):
+            for i in range(4):
+                for c in range(rows // 128):
+                    cut = slice(c * 128, (c + 1) * 128)
+                    row = index[i : i + 1, cut] if kind == 0 else index[i, :, cut]
+                    r.idx[core, kind * 4 + i, c] = row
+        r.par[core, 0:1, :] = jnp.zeros((1, width), f32)
+        r.par[core, 0:1, :cols] = r.qv_in[0:1]
+        r.par[core, 0:1, 2 * cols : 3 * cols] = r.qv_in[1:2]
+        for first, value in ((1, r.bo_in), (2, r.norm1_in), (4, r.bu_in), (5, r.bd_in), (6, r.norm2_in)):
+            r.par[core, first : first + value.shape[0], :] = value[...]
         r.vec[...] = jnp.zeros(r.vec.shape, f32)
         barrier = pltpu.get_barrier_semaphore()
         pl.semaphore_signal(barrier, inc=1, device_id=other, device_id_type=MESH)
@@ -158,19 +171,50 @@
         loop(n_z - 1, greet_z)
         loop(n_t - 1, greet_t)
         pl.semaphore_wait(barrier, n_z + n_t - 1)
-        for i in (4, 5, 0, 1, 2, 3):
+        for i in (4, 5, 0, 1):
+            swap(i).start()
+        for k in range(1, n_t):
+            wo_copy(k).start()
+        for i in (2, 3):
             swap(i).start()
         swap(4).wait()
         swap(5).wait()
 
+    def wo_copy(k):
+        return remote(
+            r.wo_in, r.wo.at[core, t], (r.wt_s.at[k - 1], r.wt_r.at[k - 1]),
+            {"tensor": lax.rem(t + k, n_t)},
+        )
+
+    def wo_on_copy(k):
+        slab = r.wo.at[core, lax.rem(t - k + n_t, n_t)]
+        return remote(slab, slab, (r.wc_s.at[k - 1], r.wc_r.at[k - 1]), other)
+
+    def out_weight_on(l, m):
+        load(5).wait()
+        for k in range(1, n_t):
+            wo_copy(k).wait_recv()
+            wo_on_copy(k).start()
+
+    asked = set()
+
     def need_weight(layer, i):
-        @pl.when(core == layer)
-        def _():
-            load(4 + i).wait()
+        if (layer, i) in asked:
+            return
+        asked.add((layer, i))
+
+        if i != 1:
+
+            @pl.when(core == layer)
+            def _():
+                load(4 + i).wait()
 
         @pl.when(core != layer)
         def _():
             swap(i).wait_recv()
+            if i == 1:
+                for k in range(1, n_t):
+                    wo_on_copy(k).wait_recv()
 
     def index_cut(kind, layer, m, first, count):
         cuts = [
@@ -229,13 +273,13 @@
         @pl.when(role == 1)
         def _():
             r.sum_src[m, 1] = part[:, left].astype(bf16)
-            r.sum_keep[m, 1] = part[:, right]
+            r.sum_keep[m, 1] = part[:, right].astype(bf16)
             sum_copy(m, 1).start()
 
         @pl.when(role == 2)
         def _():
             r.sum_src[m, 3] = part[:, right].astype(bf16)
-            r.sum_keep[m, 0] = part[:, left]
+            r.sum_keep[m, 0] = part[:, left].astype(bf16)
             sum_copy(m, 3).start()
 
         @pl.when(role == 3)
@@ -247,10 +291,10 @@
 
     def sum_mid(m):
         sum_copy(m, 0).wait_recv()
-        r.sum_src[m, 4] = (r.sum_keep[m, 0] + r.sum_dst[m, 0].astype(f32)).astype(bf16)
+        r.sum_src[m, 4] = (r.sum_keep[m, 0].astype(f32) + r.sum_dst[m, 0].astype(f32)).astype(bf16)
         sum_copy(m, 4).start()
         sum_copy(m, 2).wait_recv()
-        r.sum_src[m, 5] = (r.sum_keep[m, 1] + r.sum_dst[m, 2].astype(f32)).astype(bf16)
+        r.sum_src[m, 5] = (r.sum_keep[m, 1].astype(f32) + r.sum_dst[m, 2].astype(f32)).astype(bf16)
         sum_copy(m, 5).start()
 
     def sum_take(m):
@@ -271,39 +315,49 @@
         return rows_at(t + lax.rem(role, 2) * step_x + (role // 2) * step_y, own)
 
     def gather_copy(kind, m, j, buf):
-        if j < 2:
-            here = mine
-        elif j == 2:
-            here = pl.ds(pl.multiple_of(t_x * own, own), own // 2)
-        else:
-            here = pl.ds(pl.multiple_of(t_y * own + own // 2, own // 2), own // 2)
+        first = (t, t, t, t, t_x, t_y)[j] * own
+        low = j in (1, 2, 5)
+        here = pl.ds(pl.multiple_of(first + (own // 2 if low else 0), own // 2), own // 2)
         return remote(
             buf.at[here], buf.at[here], (r.gather_s.at[kind, m, j], r.gather_r.at[kind, m, j]),
-            {"tensor": t_x if j in (0, 3) else t_y},
+            {"tensor": t_x if j in (0, 1, 5) else t_y},
         )
 
     def gather_start(kind, m, buf):
-        gather_copy(kind, m, 0, buf).start()
-        gather_copy(kind, m, 1, buf).start()
+        for j in (0, 2, 1, 3):
+            gather_copy(kind, m, j, buf).start()
 
     def gather_on(kind, m, buf):
         gather_copy(kind, m, 0, buf).wait_recv()
-        gather_copy(kind, m, 2, buf).start()
-        gather_copy(kind, m, 1, buf).wait_recv()
-        gather_copy(kind, m, 3, buf).start()
+        gather_copy(kind, m, 4, buf).start()
+        gather_copy(kind, m, 2, buf).wait_recv()
+        gather_copy(kind, m, 5, buf).start()
+
+    def gather_near(kind, m, buf, j):
+        gather_copy(kind, m, j, buf).wait_recv()
 
     def gather_far(kind, m, buf):
-        gather_copy(kind, m, 2, buf).wait_recv()
-        gather_copy(kind, m, 3, buf).wait_recv()
+        gather_copy(kind, m, 4, buf).wait_recv()
+        gather_copy(kind, m, 5, buf).wait_recv()
+
+    def gather_rest(kind, m, buf):
+        for j in (1, 3, 4, 5):
+            gather_copy(kind, m, j, buf).wait_recv()
+        gather_sent(kind, m, buf)
 
     def gather_sent(kind, m, buf):
-        for j in range(4):
+        for j in range(6):
             gather_copy(kind, m, j, buf).wait_send()
 
     def gather_step(kind, m, role, buf):
         @pl.when(role == 1)
         def _():
             gather_on(kind, m, buf)
+            gather_near(kind, m, buf, 1)
+
+        @pl.when(role == 2)
+        def _():
+            gather_near(kind, m, buf, 3)
 
         @pl.when(role == 3)
         def _():
@@ -334,8 +388,7 @@
             out_away(kind, m, src, out).wait_send()
 
     def project(l, m):
-        if m == 0:
-            need_weight(l, 0)
+        need_weight(l, 0)
         if l == 0:
             load(m).wait()
 
@@ -346,7 +399,7 @@
             pick = (numbers == index_cut(1, l, m, cc * chunk_rows, chunk_rows)).astype(bf16)
             moved = tn(pick, r.x[m]).astype(bf16)
             r.xp[l, m, here] = moved
-            r.zs[m, here] = (nn(moved, r.wa[l]) + par(l, 0, 3 * cols)).astype(bf16)
+            r.zs[m, here] = (nt(moved, r.wa[l]) + par(l, 0, 3 * cols)).astype(bf16)
             z_send(0, m, cc, r.zs.at[m], r.zr.at[m])
 
         loop(chunks, chunk)
@@ -376,7 +429,7 @@
                 probs.append(prob.astype(bf16))
             r.entropy[l, m, pl.ds(c, 1)] = log_row
             mixed = nn(jnp.concatenate(probs, axis=1), by_head(values, heads))
-            r.mixc[m, here] = mixed.astype(bf16)
+            r.dmt[m, here] = mixed.astype(bf16)
 
         loop(rows // CLUSTER, cluster)
 
@@ -384,41 +437,46 @@
             cc = z_chunk(kk)
             here = rows_at(cc, chunk_rows)
             one_hot = place_rows(index_row(2, l, m), cc * chunk_rows, chunk_rows)
-            r.ms_src[m, here] = nn(one_hot, r.mixc[m]).astype(bf16)
-            z_send(1, m, cc, r.ms_src.at[m], r.ms.at[l, m])
+            r.dmr[m, here] = nn(one_hot, r.dmt[m]).astype(bf16)
+            z_send(1, m, cc, r.dmr.at[m], r.ms.at[m])
 
         loop(chunks, home)
-        here = rows_at(z, piece)
-        r.ms[l, m, here] = r.ms_src[m, here]
+        keep_piece(r.dmr, r.ms, m)
+
+    def heads_copy(l, m, k):
+        peer = lax.rem(t + k, n_t)
+        return remote(
+            r.ms.at[m, rows_at(peer, own)], r.mt.at[l, m, t],
+            (r.ta_s.at[m, k - 1], r.ta_r.at[m, k - 1]), {"tensor": peer},
+        )
 
     def out_project(l, m):
-        if m == 0:
-            need_weight(l, 1)
-        z_wait(1, m, r.ms_src.at[m], r.ms.at[l, m])
-
-        def part(kk):
-            role = 3 - kk
-            sum_put(m, role, nn(r.ms[l, m, role_rows(role)], r.wo[l]))
-
-        loop(n_t, part)
+        z_wait(1, m, r.dmr.at[m], r.ms.at[m])
+        for k in (2, 1, 3):
+            heads_copy(l, m, k).start()
+        r.mt[l, m, t] = r.ms[m, mine]
 
     def middle(l, m):
         sum_mid(m)
 
     def first_norm(l, m):
-        total = sum_take(m) + par(l, 1)
-        normed, inverse = normalise(r.xp[l, m, mine].astype(f32) + total)
+        need_weight(l, 1)
+        for k in range(1, n_t):
+            heads_copy(l, m, k).wait()
+        total = r.xp[l, m, mine].astype(f32) + par(l, 1)
+        for s in range(n_t):
+            total = total + nn(r.mt[l, m, s], r.wo[l, s])
+        normed, inverse = normalise(total)
         hidden = normed * par(l, 2) + par(l, 3)
-        r.n1[l, m] = normed
+        r.n1[l, m] = normed.astype(bf16)
         r.inv1[l, m] = jnp.broadcast_to(inverse, (own, 128))
         r.hid[m] = hidden
         r.hfull[l, m, mine] = hidden.astype(bf16)
         gather_start(0, m, r.hfull.at[l, m])
 
     def feed(l, m):
-        if m == 0:
-            need_weight(l, 2)
-            need_weight(l, 3)
+        need_weight(l, 2)
+        need_weight(l, 3)
 
         def part(role):
             gather_step(0, m, role, r.hfull.at[l, m])
@@ -439,7 +497,7 @@
         gather_sent(0, m, r.hfull.at[l, m])
         total = sum_take(m) + par(l, 5)
         normed, inverse = normalise(r.hid[m] + total)
-        r.n2[l, m] = normed
+        r.n2[l, m] = normed.astype(bf16)
         r.inv2[l, m] = jnp.broadcast_to(inverse, (own, 128))
         r.ag[m, mine] = (normed * par(l, 6) + par(l, 7)).astype(bf16)
         gather_start(1, m, r.ag.at[m])
@@ -455,8 +513,7 @@
         loop(rows // 128, chunk)
 
     def out_tokens(l, m):
-        gather_far(1, m, r.ag.at[m])
-        gather_sent(1, m, r.ag.at[m])
+        gather_rest(1, m, r.ag.at[m])
         if l == 1:
             out_wait(0, 0, m, r.x.at[m], r.acts)
         to_tokens(l, m, r.x, r.ag)
@@ -471,7 +528,7 @@
         numbers = lax.broadcasted_iota(jnp.int32, (rows, own), 0)
         pick = (numbers == index_cut(1, l, m, t * own, own)).astype(bf16)
         up = tn(pick, r.g[m])
-        normed = r.n2[l, m]
+        normed = r.n2[l, m].astype(f32)
         down = norm_backward(up, normed, r.inv2[l, m][:, :1], par(l, 6))
         r.hid[m] = down
         low = down.astype(bf16)
@@ -498,46 +555,69 @@
         for i in range(2):
             gather_sent(2, i, r.db.at[i])
             add_vec(l, 6, column_sum(r.gp[l, i]))
-        up = tn(r.hfull[l, 0], r.gp[l, 0]) + tn(r.hfull[l, 1], r.gp[l, 1])
-        grad_slabs(r.gs_feed, up, slice(0, width))
-        down = tn(r.db[0], r.act[l, 0]) + tn(r.db[1], r.act[l, 1])
-        grad_slabs(r.gs_feed, down, slice(width, 2 * width))
+
+        def block(c):
+            cut = rows_at(c, 256)
+            up = tn(r.hfull[l, 0], r.gp[l, 0, :, cut]) + tn(r.hfull[l, 1], r.gp[l, 1, :, cut])
+            grad_slabs(r.gs_feed, up, cut)
+            down = tn(r.db[0], r.act[l, 0, :, cut]) + tn(r.db[1], r.act[l, 1, :, cut])
+            grad_slabs(r.gs_feed, down, pl.ds(pl.multiple_of(width + c * 256, 256), 256))
+
+        loop(width // 256, block)
         grads_send(0, l, r.gs_feed, r.gr_feed)
 
     def b_first_norm(l, m):
         up = r.hid[m] + sum_take(m)
-        normed = r.n1[l, m]
+        normed = r.n1[l, m].astype(f32)
         down = norm_backward(up, normed, r.inv1[l, m][:, :1], par(l, 2))
         r.dres[m] = down
         low = down.astype(bf16)
-        r.da[m, mine] = low
-        gather_start(3, m, r.da.at[m])
+        r.da[m] = low
+
+        def part(kk):
+            k = lax.rem(kk + 1, n_t)
+            peer = lax.rem(t + k, n_t)
+            block = nt(low, r.wo[l, peer]).astype(bf16)
+
+            @pl.when(k > 0)
+            def _():
+                r.ms[m, rows_at(peer, own)] = block
+                rows_copy(m, k).start()
+
+            @pl.when(k == 0)
+            def _():
+                r.dmt[m, mine] = block
+
+        loop(n_t, part)
         add_vec(l, 3, column_sum(up * normed))
         add_vec(l, 4, column_sum(up))
         add_vec(l, 5, column_sum(low))
 
-    def b_on(l, m):
-        gather_on(3, m, r.da.at[m])
+    def rows_copy(m, k):
+        peer = lax.rem(t + k, n_t)
+        return remote(
+            r.ms.at[m, rows_at(peer, own)], r.dmt.at[m, mine], (r.tb_s.at[m, k - 1], r.tb_r.at[m, k - 1]),
+            {"tensor": peer},
+        )
 
     def out_back(l, m):
-        gather_far(3, m, r.da.at[m])
-        gather_sent(3, m, r.da.at[m])
-
-        def chunk(kk):
-            cc = z_chunk(kk)
-            here = rows_at(cc, chunk_rows)
-            r.ms_src[m, here] = nt(r.da[m, here], r.wo[l]).astype(bf16)
-            z_send(2, m, cc, r.ms_src.at[m], r.dmr.at[m])
-
-        loop(chunks, chunk)
-        keep_piece(r.ms_src, r.dmr, m)
+        for k in range(1, n_t):
+            rows_copy(m, k).wait()
+        loop(chunks, lambda kk: z_send(2, m, z_chunk(kk), r.dmt.at[m], r.dmr.at[m]))
+        keep_piece(r.dmt, r.dmr, m)
 
     def out_weights(l, m):
-        value = tn(r.da[0], r.ms[l, 0]) + tn(r.da[1], r.ms[l, 1])
-        grad_slabs(r.gs_attn, value, slice(3 * cols, 4 * cols))
+        for s in range(n_t):
+            value = tn(r.da[0], r.mt[l, 0, s]) + tn(r.da[1], r.mt[l, 1, s])
+            r.gs_out[s] = value.reshape(n_z, width // n_z, cols).astype(bf16)
+
+        @pl.when(core != l)
+        def _():
+            for k in range(n_t):
+                out_core_copy(lax.rem(t + 1 + k, n_t)).start()
 
     def b_attend(l, m):
-        z_wait(2, m, r.ms_src.at[m], r.dmr.at[m])
+        z_wait(2, m, r.dmt.at[m], r.dmr.at[m])
 
         def cluster(c):
             here = rows_at(c, CLUSTER)
@@ -582,15 +662,17 @@
 
         def part(kk):
             role = 3 - kk
-            sum_put(m, role, nt(r.zr[m, role_rows(role)], r.wa[l]))
+            sum_put(m, role, nn(r.zr[m, role_rows(role)], r.wa[l]))
 
         loop(n_t, part)
 
     def in_weights(l, m):
         for i in range(2):
             add_vec(l, 7, column_sum(r.zr[i]))
-        value = tn(r.xp[l, 0], r.zr[0]) + tn(r.xp[l, 1], r.zr[1])
-        grad_slabs(r.gs_attn, value, slice(0, 3 * cols))
+        for first in range(0, 3 * cols, 256):
+            cut = slice(first, min(first + 256, 3 * cols))
+            value = tn(r.xp[l, 0], r.zr[0, :, cut]) + tn(r.xp[l, 1], r.zr[1, :, cut])
+            grad_slabs(r.gs_attn, value, cut)
         grads_send(1, l, r.gs_attn, r.gr_attn)
 
     def layer_input(l, m):
@@ -601,8 +683,7 @@
         gather_on(4, m, r.ag.at[m])
 
     def b_tokens(l, m):
-        gather_far(4, m, r.ag.at[m])
-        gather_sent(4, m, r.ag.at[m])
+        gather_rest(4, m, r.ag.at[m])
         if l == 0:
             out_wait(1, 1, m, r.g.at[m], r.grads)
         to_tokens(l, m, r.g, r.ag)
@@ -611,10 +692,10 @@
     def grad_core_copy(kind, k, src, dst):
         return remote(src.at[k], dst.at[k], (r.gc_s.at[kind, k], r.gc_r.at[kind, k]), other)
 
-    def grad_z_copy(kind, k, src, dst):
+    def grad_z_copy(kind, k, src, dst, lanes=slice(None)):
         peer = lax.rem(z + k, n_z)
         return remote(
-            src.at[peer], dst.at[k - 1], (r.gz_s.at[kind, k - 1], r.gz_r.at[kind, k - 1]),
+            src.at[peer, :, lanes], dst.at[k - 1, :, lanes], (r.gz_s.at[kind, k - 1], r.gz_r.at[kind, k - 1]),
             {"dp": peer},
         )
 
@@ -623,29 +704,42 @@
         def _():
             loop(n_z, lambda k: grad_core_copy(kind, lax.rem(z + 1 + k, n_z), src, dst).start())
 
-    def grads_mid(kind, l, src, came, dst):
+    def grads_add(kind, src, came, k, wait, lanes):
+        peer = lax.rem(z + k, n_z)
+        if wait:
+            grad_core_copy(kind, peer, src, came).wait_recv()
+        total = src[peer, :, lanes].astype(f32) + came[peer, :, lanes].astype(f32)
+        src[peer, :, lanes] = total.astype(bf16)
+
+    def grads_part(kind, sem, l, src, came, dst, part, wait, lanes):
         @pl.when(core == l)
         def _():
-            def one(kk):
-                k = lax.rem(kk + 1, n_z)
-                peer = lax.rem(z + k, n_z)
-                grad_core_copy(kind, peer, src, came).wait_recv()
-                src[peer] = (src[peer].astype(f32) + came[peer].astype(f32)).astype(bf16)
-
-                @pl.when(k > 0)
-                def _():
-                    grad_z_copy(kind, k, src, dst).start()
-
-            loop(n_z, one)
-
-    def grads_end(kind, l, src, came, dst, out):
+            first, last = part * (n_z - 1) // 3, (part + 1) * (n_z - 1) // 3
+
+            def one(i):
+                grads_add(kind, src, came, first + 1 + i, wait, lanes)
+                grad_z_copy(sem, first + 1 + i, src, dst, lanes).start()
+
+            loop(last - first, one)
+
+    def grads_end(kind, sems, l, src, came, dst, outs):
         @pl.when(core == l)
         def _():
-            out[...] = src[z].astype(f32)
+            lanes = src.shape[2] // len(sems)
+            for i in range(len(sems)):
+                grads_add(kind, src, came, 0, i == 0, slice(i * lanes, (i + 1) * lanes))
+            cuts, first = [], 0
+            for out in outs:
+                cuts.append(slice(first, first + out.shape[-1]))
+                first += out.shape[-1]
+            for out, cut in zip(outs, cuts):
+                out[...] = src[z, :, cut].astype(f32)
 
             def one(k):
-                grad_z_copy(kind, k + 1, src, dst).wait()
-                out[...] += dst[k].astype(f32)
+                for i, sem in enumerate(sems):
+                    grad_z_copy(sem, k + 1, src, dst, slice(i * lanes, (i + 1) * lanes)).wait()
+                for out, cut in zip(outs, cuts):
+                    out[...] += dst[k, :, cut].astype(f32)
 
             loop(n_z - 1, one)
 
@@ -653,17 +747,80 @@
         def _():
             loop(n_z, lambda k: grad_core_copy(kind, k, src, came).wait_send())
 
-    def feed_mid(l, m):
-        grads_mid(0, l, r.gs_feed, r.gr_feed, r.gz_feed)
+    def feed_part(i):
+        lanes = slice(0, width) if i % 2 == 0 else slice(width, 2 * width)
+        return lambda l, m: grads_part(
+            0, i % 2, l, r.gs_feed, r.gr_feed, r.gz_feed, i // 2, i % 2 == 0, lanes
+        )
+
+    def attn_part(i):
+        return lambda l, m: grads_part(
+            1, 2, l, r.gs_attn, r.gr_attn, r.gz_attn, i, True, slice(None)
+        )
+
+    feed_0, feed_1, feed_2, feed_3, feed_4, feed_5 = (feed_part(i) for i in range(6))
+    attn_0, attn_1, attn_2 = (attn_part(i) for i in range(3))
 
     def feed_end(l, m):
-        grads_end(0, l, r.gs_feed, r.gr_feed, r.gz_feed, r.g_feed)
-
-    def attn_mid(l, m):
-        grads_mid(1, l, r.gs_attn, r.gr_attn, r.gz_attn)
+        grads_end(0, (0, 1), l, r.gs_feed, r.gr_feed, r.gz_feed, (r.g_up, r.g_down))
 
     def attn_end(l, m):
-        grads_end(1, l, r.gs_attn, r.gr_attn, r.gz_attn, r.g_attn)
+        grads_end(1, (2,), l, r.gs_attn, r.gr_attn, r.gz_attn, tuple(r.g_attn.at[i] for i in range(3)))
+
+    def out_core_copy(s):
+        return remote(r.gs_out.at[s], r.gr_out.at[s], (r.oc_s.at[s], r.oc_r.at[s]), other)
+
+    def out_t_copy(k):
+        peer = lax.rem(t + k, n_t)
+        return remote(
+            r.gs_out.at[peer], r.gt_out.at[k - 1], (r.ot_s.at[k - 1], r.ot_r.at[k - 1]),
+            {"tensor": peer},
+        )
+
+    def out_z_copy(k):
+        peer = lax.rem(z + k, n_z)
+        return remote(
+            r.gs_out.at[t, peer], r.gz_out.at[k - 1], (r.gz_s.at[3, k - 1], r.gz_r.at[3, k - 1]),
+            {"dp": peer},
+        )
+
+    def out_sum_t(l, m):
+        @pl.when(core == l)
+        def _():
+            for kk in range(n_t):
+                k = (kk + 1) % n_t
+                s = lax.rem(t + k, n_t)
+                out_core_copy(s).wait_recv()
+                r.gs_out[s] = (r.gs_out[s].astype(f32) + r.gr_out[s].astype(f32)).astype(bf16)
+                if k > 0:
+                    out_t_copy(k).start()
+
+    def out_sum_z(l, m):
+        @pl.when(core == l)
+        def _():
+            for k in range(1, n_t):
+                out_t_copy(k).wait()
+            total = r.gs_out[t].astype(f32)
+            for k in range(1, n_t):
+                total = total + r.gt_out[k - 1].astype(f32)
+            r.gs_out[t] = total.astype(bf16)
+            loop(n_z - 1, lambda k: out_z_copy(k + 1).start())
+
+        @pl.when(core != l)
+        def _():
+            for s in range(n_t):
+                out_core_copy(s).wait_send()
+
+    def out_end(l, m):
+        @pl.when(core == l)
+        def _():
+            r.g_out[...] = r.gs_out[t, z].astype(f32)
+
+            def one(k):
+                out_z_copy(k + 1).wait()
+                r.g_out[...] += r.gz_out[k].astype(f32)
+
+            loop(n_z - 1, one)
 
     def vec_copy(l):
         return remote(r.vec.at[l], r.vec_came, (r.vc_s.at[0], r.vc_r.at[0]), other)
@@ -740,30 +897,36 @@
             entropy_copy(0, m).wait_recv()
         for i in range(4):
             swap(i).wait_send()
+        for k in range(1, n_t):
+            wo_copy(k).wait_send()
+            wo_on_copy(k).wait_send()
 
     schedule = (
-        (project, 0, 0), (attend, 0, 0), (project, 0, 1), (out_project, 0, 0), (middle, 0, 0),
-        (first_norm, 0, 0), (attend, 0, 1), (feed, 0, 0), (middle, 0, 0), (out_project, 0, 1),
-        (second_norm, 0, 0), (middle, 0, 1), (out_on, 0, 0), (first_norm, 0, 1), (out_tokens, 0, 0),
-        (project, 1, 0), (feed, 0, 1), (middle, 0, 1), (attend, 1, 0), (second_norm, 0, 1), (out_on, 0, 1),
-        (out_project, 1, 0), (out_tokens, 0, 1), (project, 1, 1), (middle, 1, 0), (first_norm, 1, 0),
-        (attend, 1, 1), (feed, 1, 0), (middle, 1, 0), (out_project, 1, 1), (second_norm, 1, 0),
-        (middle, 1, 1), (b_second_norm, 1, 0), (out_on, 1, 0), (first_norm, 1, 1), (out_tokens, 1, 0),
-        (b_feed, 1, 0), (feed, 1, 1), (middle, 1, 0), (middle, 1, 1), (b_first_norm, 1, 0),
-        (second_norm, 1, 1), (b_on, 1, 0), (b_second_norm, 1, 1), (out_on, 1, 1), (out_back, 1, 0),
-        (out_tokens, 1, 1), (b_feed, 1, 1), (middle, 1, 1), (b_attend, 1, 0), (b_first_norm, 1, 1),
-        (feed_weights, 1, 1), (b_on, 1, 1), (in_project, 1, 0), (feed_mid, 1, 0), (out_back, 1, 1),
-        (middle, 1, 0), (layer_input, 1, 0), (out_weights, 1, 1), (b_out_on, 1, 0), (b_attend, 1, 1),
-        (b_tokens, 1, 0), (b_second_norm, 0, 0), (in_project, 1, 1), (b_feed, 0, 0), (middle, 1, 1),
-        (middle, 0, 0), (in_weights, 1, 1), (vec_start, 1, 0), (layer_input, 1, 1), (b_first_norm, 0, 0),
-        (b_out_on, 1, 1), (b_on, 0, 0), (b_tokens, 1, 1), (out_back, 0, 0), (b_second_norm, 0, 1),
-        (attn_mid, 1, 0), (vec_sum_t, 1, 0), (b_feed, 0, 1), (middle, 0, 1), (b_attend, 0, 0),
-        (feed_end, 1, 0), (b_first_norm, 0, 1), (vec_sum_z, 1, 0), (feed_weights, 0, 1), (b_on, 0, 1),
-        (in_project, 0, 0), (out_back, 0, 1), (middle, 0, 0), (feed_mid, 0, 0), (layer_input, 0, 0),
-        (vec_end, 1, 0), (attn_end, 1, 0), (out_weights, 0, 1), (b_attend, 0, 1), (b_out_on, 0, 0),
-        (b_tokens, 0, 0), (in_project, 0, 1), (in_weights, 0, 1), (attn_mid, 0, 0), (middle, 0, 1),
-        (vec_start, 0, 0), (layer_input, 0, 1), (vec_sum_t, 0, 0), (b_out_on, 0, 1), (vec_sum_z, 0, 0),
-        (b_tokens, 0, 1), (feed_end, 0, 0), (vec_end, 0, 0), (attn_end, 0, 0),
+        (project, 0, 1), (attend, 0, 1), (project, 0, 0), (out_weight_on, 0, 0), (out_project, 0, 1),
+        (first_norm, 0, 1), (feed, 0, 1), (attend, 0, 0), (middle, 0, 1), (second_norm, 0, 1),
+        (out_project, 0, 0), (out_on, 0, 1), (first_norm, 0, 0), (out_tokens, 0, 1), (project, 1, 1),
+        (feed, 0, 0), (middle, 0, 0), (attend, 1, 1), (second_norm, 0, 0), (out_project, 1, 1),
+        (out_on, 0, 0), (first_norm, 1, 1), (out_tokens, 0, 0), (project, 1, 0), (feed, 1, 1), (middle, 1, 1),
+        (second_norm, 1, 1), (attend, 1, 0), (out_on, 1, 1), (b_second_norm, 1, 1), (out_tokens, 1, 1),
+        (out_project, 1, 0), (b_feed, 1, 1), (first_norm, 1, 0), (middle, 1, 1), (feed, 1, 0),
+        (b_first_norm, 1, 1), (middle, 1, 0), (out_back, 1, 1), (second_norm, 1, 0), (b_second_norm, 1, 0),
+        (b_attend, 1, 1), (out_on, 1, 0), (b_feed, 1, 0), (feed_weights, 1, 1), (middle, 1, 0),
+        (in_project, 1, 1), (b_first_norm, 1, 0), (out_weights, 1, 1), (middle, 1, 1), (out_tokens, 1, 0),
+        (out_back, 1, 0), (layer_input, 1, 1), (feed_0, 1, 1), (b_out_on, 1, 1), (b_attend, 1, 0),
+        (b_tokens, 1, 1), (b_second_norm, 0, 1), (feed_1, 1, 1), (b_feed, 0, 1), (feed_2, 1, 1),
+        (in_project, 1, 0), (in_weights, 1, 1), (feed_3, 1, 1), (middle, 0, 1), (feed_4, 1, 1),
+        (middle, 1, 0), (b_first_norm, 0, 1), (layer_input, 1, 0), (vec_start, 1, 1), (out_back, 0, 1),
+        (b_out_on, 1, 0), (feed_5, 1, 1), (out_sum_t, 1, 1), (b_tokens, 1, 0), (attn_0, 1, 1), (attn_1, 1, 1),
+        (b_second_norm, 0, 0), (attn_2, 1, 1), (b_attend, 0, 1), (vec_sum_t, 1, 1), (b_feed, 0, 0),
+        (feed_end, 1, 1), (out_sum_z, 1, 1), (middle, 0, 0), (feed_weights, 0, 1), (b_first_norm, 0, 0),
+        (out_back, 0, 0), (in_project, 0, 1), (vec_sum_z, 1, 1), (middle, 0, 1), (feed_0, 0, 1),
+        (feed_1, 0, 1), (b_attend, 0, 0), (out_end, 1, 1), (layer_input, 0, 1), (out_weights, 0, 1),
+        (feed_2, 0, 1), (feed_3, 0, 1), (out_sum_t, 0, 1), (attn_end, 1, 1), (feed_4, 0, 1),
+        (in_project, 0, 0), (b_out_on, 0, 1), (in_weights, 0, 1), (middle, 0, 0), (out_sum_z, 0, 1),
+        (attn_0, 0, 1), (vec_start, 0, 1), (attn_1, 0, 1), (attn_2, 0, 1), (vec_end, 1, 1),
+        (layer_input, 0, 0), (feed_5, 0, 1), (vec_sum_t, 0, 1), (b_tokens, 0, 1), (b_out_on, 0, 0),
+        (b_tokens, 0, 0), (out_end, 0, 1), (vec_sum_z, 0, 1), (attn_end, 0, 1), (feed_end, 0, 1),
+        (vec_end, 0, 1),
     )
     start()
     for step, layer, micro in schedule:
@@ -771,7 +934,7 @@
     finish()
 
 
-def run_layers(n_z, x, g, idx, par, wa, wo, wu, wd):
+def run_layers(n_z, x, g, small, wa, wo, wu, wd):
     micros, rows, width = x.shape
     cols, hidden = wo.shape[0], wu.shape[1]
     n_t = lax.axis_size("tensor")
@@ -780,42 +943,50 @@
     both = (2, 2, rows)
     anywhere, vmem = pl.BlockSpec(memory_space=pl.ANY), pl.BlockSpec(memory_space=pltpu.VMEM)
     ins = dict(
-        x_in=anywhere, g_in=anywhere, idx_in=vmem, par_in=vmem, wa_in=anywhere, wo_in=anywhere,
+        x_in=anywhere, g_in=anywhere, items_in=vmem, send_in=vmem, recv_in=vmem, qv_in=vmem,
+        bo_in=vmem, norm1_in=vmem, bu_in=vmem, bd_in=vmem, norm2_in=vmem, wa_in=anywhere, wo_in=anywhere,
         wu_in=anywhere, wd_in=anywhere,
     )
     outs = dict(
         acts=(anywhere, x.shape, bf16), grads=(anywhere, x.shape, bf16),
-        g_feed=(vmem, (slab, 2 * width), f32), g_attn=(vmem, (slab, width), f32),
+        g_up=(vmem, (slab, width), f32), g_down=(vmem, (slab, width), f32),
+        g_attn=(vmem, (3, slab, cols), f32),
+        g_out=(vmem, (slab, cols), f32),
         vec_out=(vmem, (8, width), f32), ent=(vmem, (micros, max(8, rows // CLUSTER), 128), f32),
     )
     sem = pltpu.SemaphoreType.DMA
     scratch = dict(
         x=((*pair, width), bf16), g=((*pair, width), bf16),
-        wa=((2, width, 3 * cols), bf16), wo=((2, cols, width), bf16),
+        wa=((2, 3 * cols, width), bf16), wo=((2, n_t, cols, width), bf16),
         wu=((2, width, hidden), bf16), wd=((2, hidden, width), bf16),
-        idx=((2, *idx.shape), jnp.int32), par=((2, *par.shape), f32),
-        xp=((*both, width), bf16), grouped=((*both, 3 * cols), bf16), ms=((*both, cols), bf16),
-        n1=((2, 2, own, width), f32), inv1=((2, 2, own, 128), f32), hfull=((*both, width), bf16),
+        idx=((2, 12, rows // 128, 1, 128), jnp.int32), par=((2, 8, width), f32),
+        xp=((*both, width), bf16), grouped=((*both, 3 * cols), bf16), ms=((*pair, cols), bf16),
+        mt=((2, 2, n_t, own, cols), bf16),
+        n1=((2, 2, own, width), bf16), inv1=((2, 2, own, 128), f32), hfull=((*both, width), bf16),
         act=((*both, hidden), bf16), gp=((*both, hidden), bf16),
-        n2=((2, 2, own, width), f32), inv2=((2, 2, own, 128), f32),
+        n2=((2, 2, own, width), bf16), inv2=((2, 2, own, 128), f32),
         entropy=((2, 2, max(8, rows // CLUSTER), 128), f32),
-        zs=((*pair, 3 * cols), bf16), zr=((*pair, 3 * cols), bf16), mixc=((*pair, cols), bf16),
-        ms_src=((*pair, cols), bf16), dmr=((*pair, cols), bf16),
+        zs=((*pair, 3 * cols), bf16), zr=((*pair, 3 * cols), bf16),
+        dmr=((*pair, cols), bf16),
         sum_src=((2, 6, own, width // 2), bf16), sum_dst=((2, 6, own, width // 2), bf16),
-        sum_keep=((2, 2, own, width // 2), f32), sum_own=((2, own, width), f32),
+        sum_keep=((2, 2, own, width // 2), bf16), sum_own=((2, own, width), f32),
         hid=((2, own, width), f32), dres=((2, own, width), f32),
-        ag=((*pair, width), bf16), db=((*pair, width), bf16), da=((*pair, width), bf16),
+        ag=((*pair, width), bf16), db=((*pair, width), bf16), da=((2, own, width), bf16),
+        dmt=((*pair, cols), bf16),
         gs_feed=((n_z, slab, 2 * width), bf16), gr_feed=((n_z, slab, 2 * width), bf16),
         gz_feed=((n_z - 1, slab, 2 * width), bf16),
-        gs_attn=((n_z, slab, width), bf16), gr_attn=((n_z, slab, width), bf16),
-        gz_attn=((n_z - 1, slab, width), bf16),
+        gs_attn=((n_z, slab, 3 * cols), bf16), gr_attn=((n_z, slab, 3 * cols), bf16),
+        gz_attn=((n_z - 1, slab, 3 * cols), bf16),
+        gs_out=((n_t, n_z, slab, cols), bf16), gr_out=((n_t, n_z, slab, cols), bf16),
+        gt_out=((n_t - 1, n_z, slab, cols), bf16), gz_out=((n_z - 1, slab, cols), bf16),
         vec=((2, 8, width), f32), vec_came=((8, width), f32), vec_t=((n_t, 8, width), f32),
         vec_z=((n_z, 8, width), f32),
     )
     sems = dict(load_sem=(8,))
     for name, shape in dict(
-        swap=(6,), z=(4, 2, n_z - 1), sum=(2, 6), gather=(5, 2, 4), out=(2, 2), gc=(2, n_z),
-        gz=(2, n_z - 1), vc=(1,), vt=(n_t - 1,), vz=(n_z - 1,), en=(2,),
+        swap=(6,), z=(4, 2, n_z - 1), sum=(2, 6), gather=(5, 2, 6), out=(2, 2), gc=(2, n_z),
+        gz=(4, n_z - 1), vc=(1,), vt=(n_t - 1,), vz=(n_z - 1,), en=(2,),
+        wt=(n_t - 1,), wc=(n_t - 1,), ta=(2, n_t - 1), tb=(2, n_t - 1), oc=(n_t,), ot=(n_t - 1,),
     ).items():
         sems[name + "_s"] = shape
         sems[name + "_r"] = shape
@@ -834,7 +1005,7 @@
             collective_id=0, has_side_effects=True, vmem_limit_bytes=VMEM_LIMIT
         ),
         name="layers",
-    )(x, g, idx, par, wa, wo, wu, wd)
+    )(x, g, *small, wa, wo, wu, wd)
 
 
 def shards(
@@ -848,27 +1019,22 @@
     heads = cols // HEAD_DIM
     clusters = rows // CLUSTER
 
-    idx = jnp.concatenate(
-        [items[0], send_order[0, :, 0], recv_order[0, :, 0], jnp.zeros((4, rows), jnp.int32)]
-    ).reshape(16, rows // 128, 1, 128)
-    ba = jnp.concatenate(
-        [qv_bias[0, 0], jnp.zeros((cols,), f32), qv_bias[0, 1], jnp.zeros((width - 3 * cols,), f32)]
+    small = (
+        items[0], send_order[0], recv_order[0], qv_bias[0], out_bias, norm_first[0], up_bias,
+        down_bias, norm_second[0],
     )
-    par = jnp.concatenate(
-        [ba[None], out_bias, norm_first[0], up_bias, down_bias, norm_second[0]]
-    )
-    acts, grads, g_feed, g_attn, vec, ent = run_layers(
-        n_z, inputs, out_grad, idx, par, attn_weight[0].reshape(width, 3 * cols), out_weight[0],
-        up_weight[0], down_weight[0],
+    wa = jnp.transpose(attn_weight[0], (1, 2, 0)).reshape(3 * cols, width)
+    acts, grads, g_up, g_down, g_attn, g_out, vec, ent = run_layers(
+        n_z, inputs, out_grad, small, wa, out_weight[0], up_weight[0], down_weight[0]
     )
     item_numbers = jnp.arange(ITEMS, dtype=jnp.int32)
     grid = items[0].reshape(micros, clusters, CLUSTER)
     occupancy = jnp.sum((grid[..., None] == item_numbers).astype(f32), axis=2)
     results = (
         acts, grads.astype(f32), ent[:, :clusters, :heads], occupancy,
-        g_attn[:, : 3 * cols].reshape(-1, 3, cols),
-        jnp.stack([vec[7, :cols], vec[7, 2 * cols : 3 * cols]]), g_attn[:, 3 * cols :].T,
-        vec[5], vec[3:5], g_feed[:, :width], vec[6], g_feed[:, width:].T, vec[2], vec[0:2],
+        jnp.transpose(g_attn, (1, 0, 2)),
+        jnp.stack([vec[7, :cols], vec[7, 2 * cols : 3 * cols]]), g_out.T,
+        vec[5], vec[3:5], g_up, vec[6], g_down.T, vec[2], vec[0:2],
     )
     return tuple(value[None] for value in results)
 

time: 435 us -> 378 us (0.87); the launches traced: 429 us -> 377 us
  Pallas kernels: 401 us -> 358 us
  local copies, waits for them, and re-layouts: 19.8 us -> 12.2 us
    pallas_call x1, Pallas kernels: 401 us -> 358 us  [run_layers(): pl.pallas_call(functools.partial(layers_kernel, n_z, n_t, rows, width, co...]
    slice x3 -> x0, local copies, waits for them, and re-layouts: 4.81 us -> none  [the longest x2 4.05 us: shards(): g_attn[:, :3 * cols].reshape(-1, 3, cols)]
where the time goes in v3:
time: 378 us; the launch traced here: 377 us
  Pallas kernels  358 us (95%)
  local copies, waits for them, and re-layouts  12.2 us (3%)
  other arithmetic  5.97 us (2%)
    pallas_call x1, Pallas kernels, run_layers(): pl.pallas_call(functools.partial(layers_kernel, n_z, n_t, rows, width, co...  358 us

profile of v3, /device:TPU:0, one launch (start us, length us, event | category | flops | bytes accessed | tf_op | source)
XLA Modules:
  0.0 376.7 jit_solution(3216753904921173963)
XLA Ops:
  0.6 0.7 eq.15
  1.4 0.1 convert_reduce_fusion
  1.5 0.7 copy.32
  2.2 357.6 %layers.1 = (bf16[4,512,768]{2,1,0:T(8,128)(2,1)}, bf16[4,512,768]{2,1,0:T(8,128)(2,1)}, f32[192,768]{1,0:T(8,128)}, f32[192,768]{1,0:T(8,128)}, f32[3,192,192]{...) custom-call(bf16[4,512,768]{2,1,0:T(8,128)(2,1)} %refs_0_.1, ...), custom_call_target="tpu_custom_call" | custom-call | tf_op jit(solution)/shard_map/layers/pallas_call | solution.py:995
  359.8 0.7 fusion.1
  360.5 0.6 maximum_bitcast_fusion
  361.1 0.7 slice.24
  361.8 0.7 copy.31
  362.5 1.4 fusion
  363.9 1.4 slice_bitcast_fusion
  365.4 1.7 copy.33
  367.1 0.0 copy-start
  367.1 5.3 %bitcast_convert_fusion = f32[1,4,512,768]{3,2,1,0:T(8,128)} fusion(bf16[4,512,768]{2,1,0:T(8,128)(2,1)} %get-tuple-element.23), kind=kLoop, calls=%fused_computation | loop fusion | flops 1572864 | bytes 9437184 | tf_op jit(solution)/shard_map/broadcast_in_dim | solution.py:1039
  372.4 0.0 copy-done
  372.4 0.0 copy-start.3
  372.4 0.0 copy-start.2
  372.4 0.0 copy-start.1
  372.4 1.7 copy.38
  374.0 0.0 copy-done.3
  374.0 0.8 copy.39
  374.9 0.0 copy-done.2
  374.9 0.8 copy.40
  375.7 0.0 copy-done.1
  375.7 0.8 copy.41
Async XLA Ops:
  367.1 5.3 %copy-start = (bf16[4,512,768]{2,1,0:T(8,128)(2,1)S(1)}, bf16[4,512,768]{2,1,0:T(8,128)(2,1)}, u32[]{:S(2)}) copy-start(bf16[4,512,768]{2,1,0:T(8,128)(2,1)} %get-tuple-element.22) | copy-start | bytes 9437188
  372.4 1.7 copy-start.3
  372.4 2.5 copy-start.2
  372.4 3.3 copy-start.1
